TPU v7x, 128 devices: a whole 4x4x4 slice. The times are simulated.
128 devices in a mesh: row: 8 (over z, x_hi), col: 16 (over x_lo, y, core).
Axes of the slice: x: 4 (x_hi: 2, x_lo: 2; x = x_hi * 2 + x_lo), y: 4, z: 4, core: 2. Of those that a mesh axis runs over, the one named last changes fastest.
Arguments:
- activations: bfloat16 [512, 512, 384], P('row', 'col'), may hold values from -6 to 6
- cotangent: bfloat16 [512, 512, 384], P('row', 'col'), may hold values from -6 to 6
- first_gain: float32 [384], replicated, may hold values from 0.1 to 1.9
- joint_weight: bfloat16 [384, 1152], replicated, may hold values from -4 to 4, as said below
- output_weight: bfloat16 [384, 384], replicated, may hold values from -0.3125 to 0.3125
- second_gain: float32 [384], replicated, may hold values from 0.1 to 1.9
- expand_weight: bfloat16 [384, 1536], replicated, may hold values from -0.3125 to 0.3125
- reduce_weight: bfloat16 [1536, 384], replicated, may hold values from -0.15625 to 0.15625
Outputs:
- block_out: bfloat16 [512, 512, 384], P('row', 'col')
- grad_input: bfloat16 [512, 512, 384], P('row', 'col')
- grad_joint: float32 [384, 1152], replicated
- grad_project: float32 [384, 384], replicated
- grad_expand: float32 [384, 1536], replicated
- grad_reduce: float32 [1536, 384], replicated
- grad_first_gain: float32 [384], replicated
- grad_second_gain: float32 [384], replicated
Inputs may be any that keep to these rules, and one draw needn't show every extreme that they name: `joint_weight`: Queries, keys and values side by side along the columns, each 384 wide, heads of 32 consecutive columns.
All inputs are finite; a program needn't handle non-finite values.
Results may differ from a plain program's by a relative error of at most 0.014.
The roundings to bfloat16 on the way count: a program that leaves them out, or rounds other values in their place, can miss the bound.
Values may be sent and summed in bfloat16 or wider, within the bound.
A program may use at most 192 MiB of HBM per device.

v0:
```python
import jax
import jax.numpy as jnp
from jax import lax
from jax.sharding import PartitionSpec as P

HEADS = 12
GRID = 16


EPSILON = 1e-05
SQRT_HALF = 0.7071067811865476
INV_ROOT_TAU = 0.3989422804014327


def cut_along(array, dim, size):
    dims = array.shape
    blocks = array.reshape(*dims[:dim], size, dims[dim] // size, *dims[dim + 1 :])
    return jnp.moveaxis(blocks, dim, 0)


def in_order(blocks, dim):
    blocks = jnp.moveaxis(blocks, 0, dim)
    dims = blocks.shape
    return blocks.reshape(*dims[:dim], dims[dim] * dims[dim + 1], *dims[dim + 2 :])


def exchange_both(array, axis, axes, splits, concats):
    sizes = [lax.axis_size(a) for a in axes]
    blocks = cut_along(array, splits[0], sizes[0])
    blocks = jnp.moveaxis(cut_along(blocks, splits[1] + 1, sizes[1]), 0, 1)
    inside = blocks.shape[2:]
    blocks = blocks.reshape(-1, *inside)
    blocks = lax.all_to_all(blocks, axis, split_axis=0, concat_axis=0, tiled=True)
    blocks = in_order(blocks.reshape(*sizes, *inside), concats[0] + 1)
    return in_order(blocks, concats[1])


def normalize(values):
    center = values - jnp.mean(values, axis=-1, keepdims=True)
    inv_std = lax.rsqrt(jnp.mean(center * center, axis=-1, keepdims=True) + EPSILON)
    return (center * inv_std, inv_std)


def norm_back(grad_norm, gain_vec, normed, inv_std):
    scaled = grad_norm * gain_vec
    return inv_std * (
        scaled
        - jnp.mean(scaled, axis=-1, keepdims=True)
        - normed * jnp.mean(scaled * normed, axis=-1, keepdims=True)
    )


def gelu_value(pre_act):
    return 0.5 * pre_act * (1.0 + jax.scipy.special.erf(pre_act * SQRT_HALF))


def gelu_slope(pre_act):
    return (
        0.5 * (1.0 + jax.scipy.special.erf(pre_act * SQRT_HALF))
        + pre_act * jnp.exp(-0.5 * pre_act * pre_act) * INV_ROOT_TAU
    )


def project_rows(inputs, gain_vec, weight):
    normed, inv_std = normalize(inputs)
    scaled = (normed * gain_vec).astype(jnp.bfloat16)
    triple = jnp.dot(scaled, weight, preferred_element_type=jnp.float32).astype(jnp.bfloat16)
    return (triple, scaled, normed, inv_std)


def split_heads(rows, feature_dim):
    return rows.reshape(rows.shape[0], rows.shape[1], HEADS, feature_dim // HEADS)


def attend(triple):
    feature_dim = triple.shape[-1] // 3
    queries = split_heads(triple[..., :feature_dim], feature_dim)
    key_rows = split_heads(triple[..., feature_dim : 2 * feature_dim], feature_dim)
    value_rows = split_heads(triple[..., 2 * feature_dim :], feature_dim)
    score_scale = (feature_dim // HEADS) ** (-0.5)
    scores = (
        jnp.einsum("bqhe,bkhe->bhqk", queries, key_rows, preferred_element_type=jnp.float32)
        * score_scale
    )
    row_max = jnp.max(scores, axis=-1, keepdims=True)
    weights = jnp.exp(scores - row_max)
    weights = weights / jnp.sum(weights, axis=-1, keepdims=True)
    return (weights, queries, key_rows, value_rows, score_scale)


def attend_forward(triple):
    weights, queries, key_rows, value_rows, score_scale = attend(triple)
    mixed_rows = jnp.einsum(
        "bhqk,bkhe->bqhe",
        weights.astype(jnp.bfloat16),
        value_rows,
        preferred_element_type=jnp.float32,
    ).astype(jnp.bfloat16)
    return mixed_rows.reshape(triple.shape[0], triple.shape[1], -1)


def attend_backward(triple, grad_mixed):
    weights, queries, key_rows, value_rows, score_scale = attend(triple)
    feature_dim = triple.shape[-1] // 3
    grad_heads = split_heads(grad_mixed, feature_dim)
    grad_weights = jnp.einsum(
        "bqhe,bkhe->bhqk", grad_heads, value_rows, preferred_element_type=jnp.float32
    )
    inner_sum = jnp.sum(weights * grad_weights, axis=-1, keepdims=True)
    grad_scores = (weights * (grad_weights - inner_sum) * score_scale).astype(jnp.bfloat16)
    grad_query = jnp.einsum(
        "bhqk,bkhe->bqhe", grad_scores, key_rows, preferred_element_type=jnp.float32
    ).astype(jnp.bfloat16)
    grad_key = jnp.einsum(
        "bhqk,bqhe->bkhe", grad_scores, queries, preferred_element_type=jnp.float32
    ).astype(jnp.bfloat16)
    grad_value = jnp.einsum(
        "bhqk,bqhe->bkhe",
        weights.astype(jnp.bfloat16),
        grad_heads,
        preferred_element_type=jnp.float32,
    ).astype(jnp.bfloat16)
    shape_out = (triple.shape[0], triple.shape[1], feature_dim)
    return jnp.concatenate(
        [grad_query.reshape(shape_out), grad_key.reshape(shape_out), grad_value.reshape(shape_out)],
        axis=-1,
    )


def by_blocks(function, operands):
    groups = operands[0].shape[0]
    per_step = 2
    stacked = tuple(
        (
            operand.reshape((groups // per_step, per_step) + operand.shape[1:])
            for operand in operands
        )
    )
    result = lax.map(lambda pieces: function(*pieces), stacked)
    return result.reshape((groups,) + result.shape[2:])


def tail_back(inputs, mixed_rows, out_weight, gain_vec, up_weight, down_weight, cot_rows):
    attended = inputs + jnp.dot(mixed_rows, out_weight, preferred_element_type=jnp.float32)
    normed, inv_std = normalize(attended)
    scaled = (normed * gain_vec).astype(jnp.bfloat16)
    pre_act = jnp.dot(scaled, up_weight, preferred_element_type=jnp.float32)
    hidden = gelu_value(pre_act).astype(jnp.bfloat16)
    result = (attended + jnp.dot(hidden, down_weight, preferred_element_type=jnp.float32)).astype(
        jnp.bfloat16
    )
    grad_down = jnp.einsum("nf,nd->fd", hidden, cot_rows, preferred_element_type=jnp.float32)
    grad_hidden = jnp.einsum(
        "nd,fd->nf", cot_rows, down_weight, preferred_element_type=jnp.float32
    ).astype(jnp.bfloat16)
    grad_pre = (grad_hidden * gelu_slope(pre_act)).astype(jnp.bfloat16)
    grad_up = jnp.einsum("nd,nf->df", scaled, grad_pre, preferred_element_type=jnp.float32)
    grad_scaled = jnp.einsum("nf,df->nd", grad_pre, up_weight, preferred_element_type=jnp.float32)
    grad_gain = jnp.sum(grad_scaled * normed, axis=0)
    grad_attended = cot_rows.astype(jnp.float32) + norm_back(grad_scaled, gain_vec, normed, inv_std)
    grad_attended_b = grad_attended.astype(jnp.bfloat16)
    grad_out = jnp.einsum(
        "nd,ne->de", mixed_rows, grad_attended_b, preferred_element_type=jnp.float32
    )
    grad_mixed = jnp.einsum(
        "ne,de->nd", grad_attended_b, out_weight, preferred_element_type=jnp.float32
    ).astype(jnp.bfloat16)
    tail_grads = (grad_out, grad_gain, grad_up, grad_down)
    return (result, grad_attended, grad_mixed, tail_grads)


def head_back(normed, inv_std, scaled, gain_vec, weight, grad_triple, grad_attended):
    grad_joint = jnp.einsum("nd,nt->dt", scaled, grad_triple, preferred_element_type=jnp.float32)
    grad_scaled = jnp.einsum("nt,dt->nd", grad_triple, weight, preferred_element_type=jnp.float32)
    grad_gain = jnp.sum(grad_scaled * normed, axis=0)
    grad_input = (grad_attended + norm_back(grad_scaled, gain_vec, normed, inv_std)).astype(
        jnp.bfloat16
    )
    return (grad_input, (grad_joint, grad_gain))


def shards(
    activations,
    cotangent,
    first_gain,
    joint_weight,
    output_weight,
    second_gain,
    expand_weight,
    reduce_weight,
):
    row_devs = lax.axis_size("row")
    col_devs = lax.axis_size("col")
    tile_rows, tile_cols, channels = activations.shape
    local_rows = GRID // row_devs
    local_cols = GRID // col_devs
    stride_rows = tile_rows // local_rows
    stride_cols = tile_cols // local_cols
    part_rows = stride_rows // row_devs
    part_cols = stride_cols // col_devs
    tokens = GRID * GRID
    factor = float(tile_rows * tile_cols * row_devs * col_devs) ** (-0.5)

    def to_layout(tile):
        return tile.reshape(
            local_rows, stride_rows, local_cols, stride_cols, tile.shape[-1]
        ).transpose(1, 3, 0, 2, 4)

    def regroup(grouped):
        return grouped.reshape(part_rows, part_cols, GRID, GRID, grouped.shape[-1])

    def from_layout(arrived):
        return arrived.transpose(2, 0, 3, 1, 4).reshape(tile_rows, tile_cols, arrived.shape[-1])

    arrived_pair = (
        exchange_both(to_layout(activations), ("row", "col"), ("row", "col"), (0, 1), (2, 3)),
        exchange_both(to_layout(cotangent), ("row", "col"), ("row", "col"), (0, 1), (2, 3)),
    )
    inputs = arrived_pair[0].reshape(-1, channels).astype(jnp.float32)
    cot_rows = arrived_pair[1].reshape(-1, channels)
    triple, scaled_first, normed_first, inv_first = project_rows(inputs, first_gain, joint_weight)
    triple_grp = triple.reshape(-1, tokens, 3 * channels)
    mixed_rows = by_blocks(attend_forward, (triple_grp,)).reshape(-1, channels)
    result, grad_attended, grad_mixed, tail_grads = tail_back(
        inputs, mixed_rows, output_weight, second_gain, expand_weight, reduce_weight, cot_rows
    )
    grad_triple = by_blocks(
        attend_backward, (triple_grp, grad_mixed.reshape(-1, tokens, channels))
    ).reshape(-1, 3 * channels)
    grad_input, head_grads = head_back(
        normed_first, inv_first, scaled_first, first_gain, joint_weight, grad_triple, grad_attended
    )
    returned = (
        exchange_both(
            regroup(result.reshape(-1, tokens, channels)),
            ("row", "col"),
            ("row", "col"),
            (2, 3),
            (0, 1),
        ),
        exchange_both(
            regroup(grad_input.reshape(-1, tokens, channels)),
            ("row", "col"),
            ("row", "col"),
            (2, 3),
            (0, 1),
        ),
    )
    block_out = from_layout(returned[0])
    grad_in_tile = from_layout(returned[1])
    grad_out, grad_second, grad_up, grad_down = tail_grads
    grad_joint, grad_first = head_grads
    summed = lax.psum(
        (grad_joint, grad_out, grad_up, grad_down, grad_first, grad_second), ("row", "col")
    )
    return (block_out, grad_in_tile) + tuple((summand * factor for summand in summed))


def solution(mesh):
    placed = (P("row", "col", None), P("row", "col", None), P(), P(), P(), P(), P(), P())
    return jax.shard_map(
        shards,
        mesh=mesh,
        in_specs=placed,
        out_specs=(P("row", "col", None), P("row", "col", None), P(), P(), P(), P(), P(), P()),
        check_vma=False,
    )
```

profile of v0, /device:TPU:1, one launch (start us, length us, event | category | flops | bytes accessed | tf_op | source)
XLA Modules:
  0.0 519.4 jit_solution(16657080520869209034)
XLA Ops:
  7.2 3.1 copy.80
  10.6 2.8 copy.82
  13.3 11.5 %all-to-all-start = ((bf16[128,4,2,2,1,384]{5,3,2,1,4,0:T(2,128)(2,1)}), bf16[128,4,2,2,1,384]{5,3,2,1,4,0:T(2,128)(2,1)S(1)}, u32[]{:S(2)}, u32[]{:S(2)}) async-start(bf16[128,4,2,2,1,384]{5,3,2,1,4,0:T(2,128)(2,1)} %copy.82), calls=%async_computation | async-start | bytes 3145728 | tf_op jit(solution)/shard_map/all_to_all | solution.py:33
  24.8 3.0 copy.92
  28.2 2.8 copy.94
  30.9 18.5 %all-to-all-done = bf16[128,4,2,2,1,384]{5,3,2,1,4,0:T(2,128)(2,1)S(1)} async-done(((bf16[128,4,2,2,1,384]{5,3,2,1,4,0:T(2,128)(2,1)}), bf16[128,4,2,2,1,384]{5,3,2,1,4,0:T(2,128)(2,1)S(1)}, u32[]{:S(2)}, u32[]{:S(2)}) %all-to-all-start) | async-done | bytes 1572896 | tf_op jit(solution)/shard_map/all_to_all | solution.py:33
  50.5 4.7 all-to-all-start.2
  57.5 2.2 copy.84
  59.6 2.2 reduce_sum.117
  62.0 2.6 multiply_reduce_fusion.8
  64.7 3.4 multiply_convert_fusion.2
  68.1 11.9 %all-to-all-done.2 = bf16[128,4,2,2,1,384]{5,3,2,1,4,0:T(2,128)(2,1)S(1)} async-done(((bf16[128,4,2,2,1,384]{5,3,2,1,4,0:T(2,128)(2,1)}), bf16[128,4,2,2,1,384]{5,3,2,1,4,0:T(2,128)(2,1)S(1)}, u32[]{:S(2)}, u32[]{:S(2)}) %all-to-all-start.2) | async-done | bytes 1572896 | tf_op jit(solution)/shard_map/all_to_all | solution.py:33
  83.6 4.3 convolution_convert_fusion.1
  87.9 6.7 %copy.85 = bf16[4,2,256,1152]{2,3,1,0:T(8,128)(2,1)} copy(bf16[4,2,256,1152]{3,2,1,0:T(8,128)(2,1)} %bitcast.234) | data formatting | bytes 9437184 | tf_op jit(solution)/shard_map/while | solution.py:139
  94.5 43.1 %while.20 = (s32[]{:T(128)}, bf16[4,2,256,384]{3,2,1,0:T(8,128)(2,1)}, bf16[4,2,256,1152]{2,3,1,0:T(8,128)(2,1)}, s32[]{:T(128)}) while((s32[]{:T(128)}, bf16[4,2,256,384]{3,2,1,0:T(8,128)(2,1)}, bf16[4,2,256,1152]{2,3,1,0:T(8,128)(2,1)}, s32[]{:T(128)}) %tuple.70), condition=%wide.region_5.6_spmd, body=%wide.region_2.5_spmd.sunk | while | flops 209387776 | bytes 20496452 | solution.py:139
  96.0 4.9 fusion.125
  100.9 3.4 fusion.126
  106.8 4.9 fusion.125
  111.7 3.4 fusion.126
  117.6 4.9 fusion.125
  122.4 3.4 fusion.126
  128.3 4.9 fusion.125
  133.2 3.4 fusion.126
  137.6 3.7 fusion.61
  142.1 4.4 multiply_convert_fusion.1
  146.6 7.0 %fusion.50 = bf16[2048,1536]{1,0:T(8,128)(2,1)S(1)} fusion(f32[2048,1536]{1,0:T(8,128)S(1)} %get-tuple-element.139, bf16[2048,384]{1,0:T(8,128)(2,1)S(1)} %bitcast.215, bf16[1536,384]{1,0:T(8,128)(2,1)S(1)} %copy-done.23), kind=kOutput, calls=%fused_computation.47 | convolution fusion | flops 2453667840 | bytes 21626880 | tf_op jit(solution)/shard_map/nd,fd->nf/dot_general | solution.py:153
  153.6 4.3 fusion.55
  157.9 4.8 multiply_reduce_fusion.3
  166.5 2.3 convolution_convert_fusion.2
  168.8 4.9 fusion.64
  173.8 145.3 %while.21 = (s32[]{:T(128)}, bf16[4,2,256,1152]{3,2,1,0:T(8,128)(2,1)}, bf16[4,2,256,1152]{2,3,1,0:T(8,128)(2,1)}, bf16[4,2,256,384]{3,2,1,0:T(8,128)(2,1)}, s32[]{:T(128)}) while((s32[]{:T(128)}, bf16[4,2,256,1152]{3,2,1,0:T(8,128)(2,1)}, bf16[4,2,256,1152]{2,3,1,0:T(8,128)(2,1)}, bf16[4,2,256,384]{3,2,1,0:T(8,128)(2,1)}, s32[]{:T(128)}) %tuple.79), condition=%wide.region_14.15_spmd, body=%wide.region_10.14_spmd.sunk | while | flops 537342720 | bytes 61440080 | solution.py:139
  176.6 3.6 fusion.140
  180.2 4.9 fusion.138
  185.1 10.0 %fusion.142 = bf16[2,12,32,256]{3,2,1,0:T(8,128)(2,1)S(1)} fusion(bf16[2,256,12,32]{1,3,2,0:T(8,128)(2,1)S(1)} %bitcast.207, f32[2,12,256,256]{2,3,1,0:T(8,128)} %fusion.140, f32[2,12,256,256]{2,3,1,0:T(8,128)} %get-tuple-element.205, f32[2,12,256]{2,1,0:T(8,128)S(1)} %get-tuple-element.206), kind=kOutput, calls=%fused_computation.29.clone.1 | convolution fusion | flops 111876352 | bytes 13393920 | tf_op jit(solution)/shard_map/while/body/eval_jaxpr/bhqk,bkhe->bqhe/dot_general | solution.py:111
  195.1 9.3 %fusion.141 = bf16[2,12,32,256]{3,2,1,0:T(8,128)(2,1)S(1)} fusion(bf16[2,256,12,32]{1,3,2,0:T(8,128)(2,1)S(1)} %bitcast.205, f32[2,12,256,256]{2,3,1,0:T(8,128)} %fusion.140, f32[2,12,256,256]{2,3,1,0:T(8,128)} %get-tuple-element.205, f32[2,12,256]{2,1,0:T(8,128)S(1)} %get-tuple-element.206), kind=kOutput, calls=%fused_computation.30.clone.1 | convolution fusion | flops 111876352 | bytes 13393920 | tf_op jit(solution)/shard_map/while/body/eval_jaxpr/bhqk,bqhe->bkhe/dot_general | solution.py:114
  204.4 3.8 fusion.139
  212.8 3.6 fusion.140
  216.4 4.9 fusion.138
  221.3 10.0 %fusion.142 = bf16[2,12,32,256]{3,2,1,0:T(8,128)(2,1)S(1)} fusion(bf16[2,256,12,32]{1,3,2,0:T(8,128)(2,1)S(1)} %bitcast.207, f32[2,12,256,256]{2,3,1,0:T(8,128)} %fusion.140, f32[2,12,256,256]{2,3,1,0:T(8,128)} %get-tuple-element.205, f32[2,12,256]{2,1,0:T(8,128)S(1)} %get-tuple-element.206), kind=kOutput, calls=%fused_computation.29.clone.1 | convolution fusion | flops 111876352 | bytes 13393920 | tf_op jit(solution)/shard_map/while/body/eval_jaxpr/bhqk,bkhe->bqhe/dot_general | solution.py:111
  231.3 9.3 %fusion.141 = bf16[2,12,32,256]{3,2,1,0:T(8,128)(2,1)S(1)} fusion(bf16[2,256,12,32]{1,3,2,0:T(8,128)(2,1)S(1)} %bitcast.205, f32[2,12,256,256]{2,3,1,0:T(8,128)} %fusion.140, f32[2,12,256,256]{2,3,1,0:T(8,128)} %get-tuple-element.205, f32[2,12,256]{2,1,0:T(8,128)S(1)} %get-tuple-element.206), kind=kOutput, calls=%fused_computation.30.clone.1 | convolution fusion | flops 111876352 | bytes 13393920 | tf_op jit(solution)/shard_map/while/body/eval_jaxpr/bhqk,bqhe->bkhe/dot_general | solution.py:114
  240.6 3.8 fusion.139
  249.1 3.6 fusion.140
  252.8 4.9 fusion.138
  257.6 10.0 %fusion.142 = bf16[2,12,32,256]{3,2,1,0:T(8,128)(2,1)S(1)} fusion(bf16[2,256,12,32]{1,3,2,0:T(8,128)(2,1)S(1)} %bitcast.207, f32[2,12,256,256]{2,3,1,0:T(8,128)} %fusion.140, f32[2,12,256,256]{2,3,1,0:T(8,128)} %get-tuple-element.205, f32[2,12,256]{2,1,0:T(8,128)S(1)} %get-tuple-element.206), kind=kOutput, calls=%fused_computation.29.clone.1 | convolution fusion | flops 111876352 | bytes 13393920 | tf_op jit(solution)/shard_map/while/body/eval_jaxpr/bhqk,bkhe->bqhe/dot_general | solution.py:111
  267.7 9.3 %fusion.141 = bf16[2,12,32,256]{3,2,1,0:T(8,128)(2,1)S(1)} fusion(bf16[2,256,12,32]{1,3,2,0:T(8,128)(2,1)S(1)} %bitcast.205, f32[2,12,256,256]{2,3,1,0:T(8,128)} %fusion.140, f32[2,12,256,256]{2,3,1,0:T(8,128)} %get-tuple-element.205, f32[2,12,256]{2,1,0:T(8,128)S(1)} %get-tuple-element.206), kind=kOutput, calls=%fused_computation.30.clone.1 | convolution fusion | flops 111876352 | bytes 13393920 | tf_op jit(solution)/shard_map/while/body/eval_jaxpr/bhqk,bqhe->bkhe/dot_general | solution.py:114
  277.0 3.8 fusion.139
  285.3 3.6 fusion.140
  289.0 4.9 fusion.138
  293.9 10.0 %fusion.142 = bf16[2,12,32,256]{3,2,1,0:T(8,128)(2,1)S(1)} fusion(bf16[2,256,12,32]{1,3,2,0:T(8,128)(2,1)S(1)} %bitcast.207, f32[2,12,256,256]{2,3,1,0:T(8,128)} %fusion.140, f32[2,12,256,256]{2,3,1,0:T(8,128)} %get-tuple-element.205, f32[2,12,256]{2,1,0:T(8,128)S(1)} %get-tuple-element.206), kind=kOutput, calls=%fused_computation.29.clone.1 | convolution fusion | flops 111876352 | bytes 13393920 | tf_op jit(solution)/shard_map/while/body/eval_jaxpr/bhqk,bkhe->bqhe/dot_general | solution.py:111
  303.9 9.3 %fusion.141 = bf16[2,12,32,256]{3,2,1,0:T(8,128)(2,1)S(1)} fusion(bf16[2,256,12,32]{1,3,2,0:T(8,128)(2,1)S(1)} %bitcast.205, f32[2,12,256,256]{2,3,1,0:T(8,128)} %fusion.140, f32[2,12,256,256]{2,3,1,0:T(8,128)} %get-tuple-element.205, f32[2,12,256]{2,1,0:T(8,128)S(1)} %get-tuple-element.206), kind=kOutput, calls=%fused_computation.30.clone.1 | convolution fusion | flops 111876352 | bytes 13393920 | tf_op jit(solution)/shard_map/while/body/eval_jaxpr/bhqk,bqhe->bkhe/dot_general | solution.py:114
  313.2 3.8 fusion.139
  319.1 6.3 %fusion.63 = f32[384,1152]{1,0:T(8,128)} fusion(bf16[2048,384]{1,0:T(8,128)(2,1)} %bitcast.238, bf16[2048,1152]{1,0:T(8,128)(2,1)} %bitcast.239), kind=kOutput, calls=%fused_computation.97 | convolution fusion | flops 1811939328 | bytes 8060928 | tf_op jit(solution)/shard_map/nd,nt->dt/dot_general | solution.py:173
  326.7 7.5 %add_convert_fusion.1 = bf16[2048,384]{1,0:T(8,128)(2,1)S(1)} fusion(f32[2048,384]{1,0:T(8,128)} %copy-done.4, bf16[2048,1536]{1,0:T(8,128)(2,1)} %copy-done.7, bf16[1536,384]{1,0:T(8,128)(2,1)S(1)} %copy-done.24), kind=kOutput, calls=%fused_computation.63 | convolution fusion | flops 2417491968 | bytes 12189696 | tf_op jit(solution)/shard_map/dot_general | solution.py:149
  334.5 2.8 copy.88
  337.2 5.3 %all-to-all-start.1 = ((bf16[128,4,2,2,1,384]{5,3,2,1,4,0:T(2,128)(2,1)}), bf16[128,4,2,2,1,384]{5,3,2,1,4,0:T(2,128)(2,1)S(1)}, u32[]{:S(2)}, u32[]{:S(2)}) async-start(bf16[128,4,2,2,1,384]{5,3,2,1,4,0:T(2,128)(2,1)} %copy.88), calls=%async_computation.1 | async-start | bytes 3145728 | tf_op jit(solution)/shard_map/all_to_all | solution.py:33
  342.6 7.5 %multiply_reduce_fusion.4 = (f32[384]{0:T(512)S(1)}, f32[2048]{0:T(1024)S(1)}, f32[2048]{0:T(1024)S(1)}, f32[2048,384]{1,0:T(8,128)S(1)}) fusion(f32[16,4,2,8,2,1,384]{6,0,4,3,2,1,5:T(8,128)} %copy.84, f32[2048]{0:T(1024)S(1)} %copy-done.18, f32[2048]{0:T(1024)S(1)} %copy-done.16, f32[384]{0:T(512)S(1)} %copy-done.21, bf16[2048,1152]{1,0:T(8,128)(2,1)} %bitcast.240, ...), kind=kOutput, calls=%fused_computation.57 | convolution fusion | flops 1818226304 | bytes 11930624 | tf_op jit(solution)/shard_map/nt,dt->nd/dot_general | solution.py:174
  352.1 2.8 copy.101
  354.9 15.3 %all-to-all-done.1 = bf16[128,4,2,2,1,384]{5,3,2,1,4,0:T(2,128)(2,1)S(1)} async-done(((bf16[128,4,2,2,1,384]{5,3,2,1,4,0:T(2,128)(2,1)}), bf16[128,4,2,2,1,384]{5,3,2,1,4,0:T(2,128)(2,1)S(1)}, u32[]{:S(2)}, u32[]{:S(2)}) %all-to-all-start.1) | async-done | bytes 1572896 | tf_op jit(solution)/shard_map/all_to_all | solution.py:33
  370.2 6.1 %all-to-all-start.3 = ((bf16[128,4,2,2,1,384]{5,3,2,1,4,0:T(2,128)(2,1)}), bf16[128,4,2,2,1,384]{5,3,2,1,4,0:T(2,128)(2,1)}, u32[]{:S(2)}, u32[]{:S(2)}) async-start(bf16[128,4,2,2,1,384]{5,3,2,1,4,0:T(2,128)(2,1)} %copy.101), calls=%async_computation.3 | async-start | bytes 3145728 | tf_op jit(solution)/shard_map/all_to_all | solution.py:33
  376.3 78.1 %all-reduce = (f32[384]{0:T(512)S(1)}, f32[384]{0:T(512)S(1)}) all-reduce(f32[384]{0:T(512)S(1)} %get-tuple-element.102, f32[384]{0:T(512)S(1)} %copy-done.22), channel_id=1, replica_groups=mesh['row'=8,'col'=16] {'row','col'}, use_global_device_ids=true, to_apply=%region_22.23 | all-reduce | flops 768 | bytes 6144 | tf_op jit(solution)/shard_map/psum | solution.py:253
  457.1 2.1 copy.105
  462.2 2.1 copy.106
  464.3 40.8 %all-reduce.4.cloned.1.call-done = (f32[384,1152]{1,0:T(8,128)}, f32[384,384]{1,0:T(8,128)}, f32[384,1536]{1,0:T(8,128)}, f32[1536,384]{1,0:T(8,128)}) async-done(((f32[384,1152]{1,0:T(8,128)}, f32[384,384]{1,0:T(8,128)}, f32[384,1536]{1,0:T(8,128)}, f32[1536,384]{1,0:T(8,128)}), (f32[384,1152]{1,0:T(8,128)}, f32[384,384]{1,0:T(8,128)}, f32[384,1536]{1,0:T(8,128)}, ...) | async-done | bytes 7077904 | tf_op jit(solution)/shard_map/psum | solution.py:253
  505.1 2.9 broadcast_multiply_fusion.2
  (136 shorter events, 53.6 us)
Async XLA Ops:
  7.2 134.9 %copy-start = (bf16[384,1536]{1,0:T(8,128)(2,1)S(1)}, bf16[384,1536]{1,0:T(8,128)(2,1)}, u32[]{:S(2)}) copy-start(bf16[384,1536]{1,0:T(8,128)(2,1)} %param.18) | copy-start | bytes 3538948
  13.3 36.1 %all-to-all-start = ((bf16[128,4,2,2,1,384]{5,3,2,1,4,0:T(2,128)(2,1)}), bf16[128,4,2,2,1,384]{5,3,2,1,4,0:T(2,128)(2,1)S(1)}, u32[]{:S(2)}, u32[]{:S(2)}) async-start(bf16[128,4,2,2,1,384]{5,3,2,1,4,0:T(2,128)(2,1)} %copy.82), calls=%async_computation | async-start | bytes 3145728 | tf_op jit(solution)/shard_map/all_to_all | solution.py:33
  49.4 1.1 copy-start.9
  50.5 29.4 %all-to-all-start.2 = ((bf16[128,4,2,2,1,384]{5,3,2,1,4,0:T(2,128)(2,1)}), bf16[128,4,2,2,1,384]{5,3,2,1,4,0:T(2,128)(2,1)S(1)}, u32[]{:S(2)}, u32[]{:S(2)}) async-start(bf16[128,4,2,2,1,384]{5,3,2,1,4,0:T(2,128)(2,1)} %copy.94), calls=%async_computation.2 | async-start | bytes 3145728 | tf_op jit(solution)/shard_map/all_to_all | solution.py:33
  55.2 449.9 %all-reduce.4.cloned.1.call-start = ((), (), s32[]{:S(2)}) async-start(), calls=%async_computation.4 | async-start | bytes 14155776 | tf_op jit(solution)/shard_map/psum | solution.py:253
  59.6 5.1 copy-start.20
  62.0 19.7 %copy-start.15 = (f32[2048]{0:T(1024)}, f32[2048]{0:T(1024)S(1)}, u32[]{:S(2)}) copy-start(f32[2048]{0:T(1024)S(1)} %div.43) | copy-start | bytes 24580
  64.7 17.0 %copy-start.17 = (f32[2048]{0:T(1024)}, f32[2048]{0:T(1024)S(1)}, u32[]{:S(2)}) copy-start(f32[2048]{0:T(1024)S(1)} %rsqrt.21) | copy-start | bytes 24580
  79.9 2.5 copy-start.2
  82.4 1.2 copy-start.25
  94.5 43.1 %copy-start.13 = (bf16[384,384]{1,0:T(8,128)(2,1)S(1)}, bf16[384,384]{1,0:T(8,128)(2,1)}, u32[]{:S(2)}) copy-start(bf16[384,384]{1,0:T(8,128)(2,1)} %param.16) | copy-start | bytes 884740
  141.3 21.3 %copy-start.4 = (f32[2048,384]{1,0:T(8,128)}, f32[2048,384]{1,0:T(8,128)S(1)}, u32[]{:S(2)}) copy-start(f32[2048,384]{1,0:T(8,128)S(1)} %get-tuple-element.137) | copy-start | bytes 9437188
  141.3 0.8 copy-start.19
  142.1 4.4 copy-start.8
  142.1 4.4 copy-start.23
  146.5 22.3 %copy-start.7 = (bf16[2048,1536]{1,0:T(8,128)(2,1)}, bf16[2048,1536]{1,0:T(8,128)(2,1)S(1)}, u32[]{:S(2)}) copy-start(bf16[2048,1536]{1,0:T(8,128)(2,1)S(1)} %get-tuple-element.138) | copy-start | bytes 18874372
  162.7 2.0 copy-start.10
  164.7 4.1 copy-start.5
  325.4 1.3 copy-start.24
  334.4 8.2 %copy-start.16 = (f32[2048]{0:T(1024)S(1)}, f32[2048]{0:T(1024)}, u32[]{:S(2)}) copy-start(f32[2048]{0:T(1024)} %copy-done.15) | copy-start | bytes 24580
  334.4 8.2 %copy-start.18 = (f32[2048]{0:T(1024)S(1)}, f32[2048]{0:T(1024)}, u32[]{:S(2)}) copy-start(f32[2048]{0:T(1024)} %copy-done.17) | copy-start | bytes 24580
  334.4 8.2 %copy-start.21 = (f32[384]{0:T(512)S(1)}, f32[384]{0:T(512)}, u32[]{:S(2)}) copy-start(f32[384]{0:T(512)} %param.14) | copy-start | bytes 4612
  334.5 8.2 %copy-start.26 = (bf16[384,1152]{1,0:T(8,128)(2,1)S(1)}, bf16[384,1152]{1,0:T(8,128)(2,1)}, u32[]{:S(2)}) copy-start(bf16[384,1152]{1,0:T(8,128)(2,1)} %param.15) | copy-start | bytes 2654212
  337.2 33.0 %all-to-all-start.1 = ((bf16[128,4,2,2,1,384]{5,3,2,1,4,0:T(2,128)(2,1)}), bf16[128,4,2,2,1,384]{5,3,2,1,4,0:T(2,128)(2,1)S(1)}, u32[]{:S(2)}, u32[]{:S(2)}) async-start(bf16[128,4,2,2,1,384]{5,3,2,1,4,0:T(2,128)(2,1)} %copy.88), calls=%async_computation.1 | async-start | bytes 3145728 | tf_op jit(solution)/shard_map/all_to_all | solution.py:33
  342.6 7.5 %copy-start.3 = (f32[16,4,2,8,2,1,384]{6,0,4,3,2,1,5:T(8,128)S(1)}, f32[16,4,2,8,2,1,384]{6,0,4,3,2,1,5:T(8,128)}, u32[]{:S(2)}) copy-start(f32[16,4,2,8,2,1,384]{6,0,4,3,2,1,5:T(8,128)} %copy.84) | copy-start | bytes 9437188
  342.6 7.5 %copy-start.6 = (f32[2048,384]{1,0:T(8,128)S(1)}, f32[2048,384]{1,0:T(8,128)}, u32[]{:S(2)}) copy-start(f32[2048,384]{1,0:T(8,128)} %copy-done.5) | copy-start | bytes 9437188
  352.1 24.2 %copy-start.22 = (f32[384]{0:T(512)S(1)}, f32[384]{0:T(512)}, u32[]{:S(2)}) copy-start(f32[384]{0:T(512)} %get-tuple-element.100) | copy-start | bytes 4612
  370.2 89.0 %all-to-all-start.3 = ((bf16[128,4,2,2,1,384]{5,3,2,1,4,0:T(2,128)(2,1)}), bf16[128,4,2,2,1,384]{5,3,2,1,4,0:T(2,128)(2,1)}, u32[]{:S(2)}, u32[]{:S(2)}) async-start(bf16[128,4,2,2,1,384]{5,3,2,1,4,0:T(2,128)(2,1)} %copy.101), calls=%async_computation.3 | async-start | bytes 3145728 | tf_op jit(solution)/shard_map/all_to_all | solution.py:33
  505.1 3.0 copy-start.14
  505.1 3.8 copy-start.12
  508.1 2.5 copy-start.11
  508.9 3.1 copy-start.1
Sparse Core Ops, SparseCore 0:
  325.5 179.5 all-reduce.3
where the time goes:
time: 529 us; the launch traced here: 519 us
  matrix products  218 us (41%)
  waiting for transfers between devices  86.5 us (16%)
  blocking collectives  78.1 us (15%)
  local copies, waits for them, and re-layouts  70.6 us (13%)
  starting transfers between devices  27.6 us (5%)
  other arithmetic  22.4 us (4%)
  between operations  15 us (3%)
    psum x1, blocking collectives, shards(): lax.psum((grad_joint, grad_out, grad_up, grad_down, grad_first, grad_seco...  78.1 us
    all_to_all x4, waiting for transfers between devices, exchange_both(): lax.all_to_all(blocks, axis, split_axis=0, concat_axis=0, tiled=True)  45.7 us
    psum x1, waiting for transfers between devices, shards(): lax.psum((grad_joint, grad_out, grad_up, grad_down, grad_first, grad_seco...  40.8 us
    dot_general x4, matrix products, attend_backward(): jnp.einsum('bhqk,bkhe->bqhe', grad_scores, key_rows, preferred_element_ty...  40.1 us
    sub x8, matrix products, attend(): weights = jnp.exp(scores - row_max)  39 us
    dot_general x4, matrix products, attend_backward(): jnp.einsum('bhqk,bqhe->bkhe', grad_scores, queries, preferred_element_typ...  37.1 us
    all_to_all x4, starting transfers between devices, exchange_both(): lax.all_to_all(blocks, axis, split_axis=0, concat_axis=0, tiled=True)  27.6 us
    dot_general x4, matrix products, attend_backward(): jnp.einsum('bhqk,bqhe->bkhe', weights.astype(jnp.bfloat16), grad_heads, p...  15.2 us
  transfers between devices with their start and end apart: 5, of which 4 were waited for; matrix products, arithmetic and copies ran while one was open for 10% of the time, Pallas kernels for 0%

commit v1 on v0

--- a/solution.py
+++ b/solution.py
@@ -1,6 +1,8 @@
 import jax
 import jax.numpy as jnp
 from jax import lax
+from jax.experimental import pallas as pl
+from jax.experimental.pallas import tpu as pltpu
 from jax.sharding import PartitionSpec as P
 
 HEADS = 12
@@ -22,6 +24,57 @@
     blocks = jnp.moveaxis(blocks, 0, dim)
     dims = blocks.shape
     return blocks.reshape(*dims[:dim], dims[dim] * dims[dim + 1], *dims[dim + 2 :])
+
+
+def swap_kernel(source, arrived, send_sem, recv_sem):
+    rows = lax.axis_size("row")
+    cols = lax.axis_size("col")
+    count = rows * cols
+    me = lax.axis_index("row") * cols + lax.axis_index("col")
+    barrier = pltpu.get_barrier_semaphore()
+
+    def place(step):
+        peer = lax.rem(me + step, count)
+        return peer, (peer // cols, lax.rem(peer, cols))
+
+    def greet(step, carry):
+        pl.semaphore_signal(
+            barrier, inc=1, device_id=place(step)[1], device_id_type=pl.DeviceIdType.MESH
+        )
+        return carry
+
+    def send(step, carry):
+        peer, where = place(step)
+        pltpu.make_async_remote_copy(
+            src_ref=source.at[peer],
+            dst_ref=arrived.at[me],
+            send_sem=send_sem,
+            recv_sem=recv_sem,
+            device_id=where,
+            device_id_type=pl.DeviceIdType.MESH,
+        ).start()
+        return carry
+
+    lax.fori_loop(1, count, greet, 0)
+    pl.semaphore_wait(barrier, count - 1)
+    lax.fori_loop(1, count, send, 0)
+    arrived[me] = source[me]
+    others = pl.ds(0, count - 1)
+    pltpu.make_async_copy(source.at[others], source.at[others], send_sem).wait()
+    pltpu.make_async_copy(arrived.at[others], arrived.at[others], recv_sem).wait()
+
+
+def swap_blocks(blocks):
+    return pl.pallas_call(
+        swap_kernel,
+        out_shape=jax.ShapeDtypeStruct(blocks.shape, blocks.dtype),
+        in_specs=[pl.BlockSpec(memory_space=pltpu.VMEM)],
+        out_specs=pl.BlockSpec(memory_space=pltpu.VMEM),
+        scratch_shapes=[pltpu.SemaphoreType.DMA, pltpu.SemaphoreType.DMA],
+        compiler_params=pltpu.CompilerParams(
+            collective_id=0, has_side_effects=True, vmem_limit_bytes=32 * 2**20
+        ),
+    )(blocks)
 
 
 def exchange_both(array, axis, axes, splits, concats):
@@ -30,7 +83,8 @@
     blocks = jnp.moveaxis(cut_along(blocks, splits[1] + 1, sizes[1]), 0, 1)
     inside = blocks.shape[2:]
     blocks = blocks.reshape(-1, *inside)
-    blocks = lax.all_to_all(blocks, axis, split_axis=0, concat_axis=0, tiled=True)
+    shape = blocks.shape
+    blocks = swap_blocks(blocks.reshape(shape[0], 16, shape[-1])).reshape(shape)
     blocks = in_order(blocks.reshape(*sizes, *inside), concats[0] + 1)
     return in_order(blocks, concats[1])
 

time: 529 us -> 572 us (1.081)
  Pallas kernels: 0 us -> 134 us
  waiting for transfers between devices: 86.5 us -> 14.8 us
  local copies, waits for them, and re-layouts: 70.6 us -> 99.6 us
  starting transfers between devices: 27.6 us -> 0.04 us
  blocking collectives: 78.1 us -> 64.8 us
    pallas_call x0 -> x4, Pallas kernels: none -> 134 us  [swap_blocks(): pl.pallas_call(swap_kernel, out_shape=jax.ShapeDtypeStruct(blocks.shape,...]
    all_to_all x4 -> x0, waiting for transfers between devices: 45.7 us -> none  [exchange_both(): lax.all_to_all(blocks, axis, split_axis=0, concat_axis=0, tiled=True)]
    another operation x0 -> x10, local copies, waits for them, and re-layouts: none -> 28.3 us  [the longest x4 15.1 us: exchange_both(): blocks = swap_blocks(blocks.reshape(shape[0], 16, shape[-1])).reshape(shape)]
    all_to_all x4 -> x0, starting transfers between devices: 27.6 us -> none  [exchange_both(): lax.all_to_all(blocks, axis, split_axis=0, concat_axis=0, tiled=True)]
    psum x1, waiting for transfers between devices: 40.8 us -> 14.8 us  [shards(): lax.psum((grad_joint, grad_out, grad_up, grad_down, grad_first, grad_seco...]
    psum x1, blocking collectives: 78.1 us -> 64.8 us  [shards(): lax.psum((grad_joint, grad_out, grad_up, grad_down, grad_first, grad_seco...]
    reshape x4 -> x0, local copies, waits for them, and re-layouts: 11 us -> none  [exchange_both(): blocks = blocks.reshape(-1, *inside)]
    convert_element_type x1 -> x2, local copies, waits for them, and re-layouts: 2.17 us -> 9.52 us  [shards(): inputs = arrived_pair[0].reshape(-1, channels).astype(jnp.float32)]
  transfers between devices with their start and end apart: 5 -> 1, of which waited for: 4 -> 1; matrix products, arithmetic and copies ran while one was open for 10% -> 7% of each run, Pallas kernels for 0% -> 12%
where the time goes in v1:
time: 572 us; the launch traced here: 567 us
  matrix products  217 us (38%)
  Pallas kernels  134 us (23%)
  local copies, waits for them, and re-layouts  99.6 us (17%)
  blocking collectives  64.8 us (11%)
  other arithmetic  22 us (4%)
  waiting for transfers between devices  14.8 us (3%)
  between operations  14.8 us (3%)
    pallas_call x4, Pallas kernels, swap_blocks(): pl.pallas_call(swap_kernel, out_shape=jax.ShapeDtypeStruct(blocks.shape,...  134 us
    psum x1, blocking collectives, shards(): lax.psum((grad_joint, grad_out, grad_up, grad_down, grad_first, grad_seco...  64.8 us
    dot_general x4, matrix products, attend_backward(): jnp.einsum('bhqk,bkhe->bqhe', grad_scores, key_rows, preferred_element_ty...  40.1 us
    sub x8, matrix products, attend(): weights = jnp.exp(scores - row_max)  39 us
    dot_general x4, matrix products, attend_backward(): jnp.einsum('bhqk,bqhe->bkhe', grad_scores, queries, preferred_element_typ...  37.1 us
    dot_general x4, matrix products, attend_backward(): jnp.einsum('bhqk,bqhe->bkhe', weights.astype(jnp.bfloat16), grad_heads, p...  15.2 us
    another operation x4, local copies, waits for them, and re-layouts, exchange_both(): blocks = swap_blocks(blocks.reshape(shape[0], 16, shape[-1])).reshape(shape)  15.1 us
    psum x1, waiting for transfers between devices, shards(): lax.psum((grad_joint, grad_out, grad_up, grad_down, grad_first, grad_seco...  14.8 us
  transfers between devices with their start and end apart: 1, of which 1 were waited for; matrix products, arithmetic and copies ran while one was open for 7% of the time, Pallas kernels for 12%

profile of v1, /device:TPU:1, one launch (start us, length us, event | category | flops | bytes accessed | tf_op | source)
XLA Modules:
  0.0 567.4 jit_solution(8920599176555421981)
XLA Ops:
  7.2 3.1 copy.48
  10.3 2.4 copy.49
  12.7 4.1 reshape_reshape.48.source
  16.8 36.9 %shard_map.143 = bf16[128,16,384]{2,1,0:T(8,128)(2,1)S(1)} custom-call(bf16[128,16,384]{2,1,0:T(8,128)(2,1)S(1)} %reshape_reshape.48.source), custom_call_target="tpu_custom_call" | custom-call | tf_op jit(solution)/shard_map/pallas_call | solution.py:68
  54.9 4.9 reshape.192
  59.8 4.7 copy.50
  66.8 2.6 multiply_reduce_fusion.8
  69.5 3.2 multiply_convert_fusion.2
  74.4 2.4 copy.57
  76.8 3.7 reshape_reshape.55.source
  80.4 30.6 %shard_map.145 = bf16[128,16,384]{2,1,0:T(8,128)(2,1)S(1)} custom-call(bf16[128,16,384]{2,1,0:T(8,128)(2,1)S(1)} %reshape_reshape.55.source), custom_call_target="tpu_custom_call" | custom-call | tf_op jit(solution)/shard_map/pallas_call | solution.py:68
  112.2 3.7 reshape_reshape.56
  119.5 4.3 convolution_convert_fusion.1
  123.8 6.7 %copy.51 = bf16[4,2,256,1152]{2,3,1,0:T(8,128)(2,1)} copy(bf16[4,2,256,1152]{3,2,1,0:T(8,128)(2,1)} %bitcast.229) | data formatting | bytes 9437184 | tf_op jit(solution)/shard_map/while | solution.py:193
  130.5 43.1 %while.20 = (s32[]{:T(128)}, bf16[4,2,256,384]{3,2,1,0:T(8,128)(2,1)}, bf16[4,2,256,1152]{2,3,1,0:T(8,128)(2,1)}, s32[]{:T(128)}) while((s32[]{:T(128)}, bf16[4,2,256,384]{3,2,1,0:T(8,128)(2,1)}, bf16[4,2,256,1152]{2,3,1,0:T(8,128)(2,1)}, s32[]{:T(128)}) %tuple.65), condition=%wide.region_5.6_spmd, body=%wide.region_2.5_spmd.sunk | while | flops 209387776 | bytes 20496452 | solution.py:193
  131.9 4.9 fusion.125
  136.8 3.4 fusion.126
  142.7 4.9 fusion.125
  147.6 3.4 fusion.126
  153.5 4.9 fusion.125
  158.4 3.4 fusion.126
  164.2 4.9 fusion.125
  169.1 3.4 fusion.126
  173.6 3.7 fusion.61
  178.0 4.4 multiply_convert_fusion.1
  182.5 6.8 %fusion.50 = bf16[2048,1536]{1,0:T(8,128)(2,1)S(1)} fusion(f32[2048,1536]{1,0:T(8,128)S(1)} %get-tuple-element.117, bf16[2048,384]{1,0:T(8,128)(2,1)S(1)} %bitcast.216, bf16[1536,384]{1,0:T(8,128)(2,1)S(1)} %copy-done.27), kind=kOutput, calls=%fused_computation.47 | convolution fusion | flops 2453667840 | bytes 21626880 | tf_op jit(solution)/shard_map/nd,fd->nf/dot_general | solution.py:207
  189.3 4.3 fusion.55
  193.6 4.8 multiply_reduce_fusion.3
  204.5 4.9 fusion.64
  209.5 145.5 %while.21 = (s32[]{:T(128)}, bf16[4,2,256,1152]{3,2,1,0:T(8,128)(2,1)}, bf16[4,2,256,1152]{2,3,1,0:T(8,128)(2,1)}, bf16[4,2,256,384]{3,2,1,0:T(8,128)(2,1)}, s32[]{:T(128)}) while((s32[]{:T(128)}, bf16[4,2,256,1152]{3,2,1,0:T(8,128)(2,1)}, bf16[4,2,256,1152]{2,3,1,0:T(8,128)(2,1)}, bf16[4,2,256,384]{3,2,1,0:T(8,128)(2,1)}, s32[]{:T(128)}) %tuple.74), condition=%wide.region_14.15_spmd, body=%wide.region_10.14_spmd.sunk | while | flops 537342720 | bytes 61440080 | solution.py:193
  212.5 3.6 fusion.140
  216.2 4.9 fusion.138
  221.1 10.0 %fusion.142 = bf16[2,12,32,256]{3,2,1,0:T(8,128)(2,1)S(1)} fusion(bf16[2,256,12,32]{1,3,2,0:T(8,128)(2,1)S(1)} %bitcast.208, f32[2,12,256,256]{2,3,1,0:T(8,128)} %fusion.140, f32[2,12,256,256]{2,3,1,0:T(8,128)} %get-tuple-element.183, f32[2,12,256]{2,1,0:T(8,128)S(1)} %get-tuple-element.184), kind=kOutput, calls=%fused_computation.29.clone.1 | convolution fusion | flops 111876352 | bytes 13393920 | tf_op jit(solution)/shard_map/while/body/eval_jaxpr/bhqk,bkhe->bqhe/dot_general | solution.py:165
  231.1 9.3 %fusion.141 = bf16[2,12,32,256]{3,2,1,0:T(8,128)(2,1)S(1)} fusion(bf16[2,256,12,32]{1,3,2,0:T(8,128)(2,1)S(1)} %bitcast.206, f32[2,12,256,256]{2,3,1,0:T(8,128)} %fusion.140, f32[2,12,256,256]{2,3,1,0:T(8,128)} %get-tuple-element.183, f32[2,12,256]{2,1,0:T(8,128)S(1)} %get-tuple-element.184), kind=kOutput, calls=%fused_computation.30.clone.1 | convolution fusion | flops 111876352 | bytes 13393920 | tf_op jit(solution)/shard_map/while/body/eval_jaxpr/bhqk,bqhe->bkhe/dot_general | solution.py:168
  240.4 3.8 fusion.139
  248.8 3.6 fusion.140
  252.4 4.9 fusion.138
  257.3 10.0 %fusion.142 = bf16[2,12,32,256]{3,2,1,0:T(8,128)(2,1)S(1)} fusion(bf16[2,256,12,32]{1,3,2,0:T(8,128)(2,1)S(1)} %bitcast.208, f32[2,12,256,256]{2,3,1,0:T(8,128)} %fusion.140, f32[2,12,256,256]{2,3,1,0:T(8,128)} %get-tuple-element.183, f32[2,12,256]{2,1,0:T(8,128)S(1)} %get-tuple-element.184), kind=kOutput, calls=%fused_computation.29.clone.1 | convolution fusion | flops 111876352 | bytes 13393920 | tf_op jit(solution)/shard_map/while/body/eval_jaxpr/bhqk,bkhe->bqhe/dot_general | solution.py:165
  267.3 9.3 %fusion.141 = bf16[2,12,32,256]{3,2,1,0:T(8,128)(2,1)S(1)} fusion(bf16[2,256,12,32]{1,3,2,0:T(8,128)(2,1)S(1)} %bitcast.206, f32[2,12,256,256]{2,3,1,0:T(8,128)} %fusion.140, f32[2,12,256,256]{2,3,1,0:T(8,128)} %get-tuple-element.183, f32[2,12,256]{2,1,0:T(8,128)S(1)} %get-tuple-element.184), kind=kOutput, calls=%fused_computation.30.clone.1 | convolution fusion | flops 111876352 | bytes 13393920 | tf_op jit(solution)/shard_map/while/body/eval_jaxpr/bhqk,bqhe->bkhe/dot_general | solution.py:168
  276.6 3.8 fusion.139
  285.1 3.6 fusion.140
  288.7 4.9 fusion.138
  293.6 10.0 %fusion.142 = bf16[2,12,32,256]{3,2,1,0:T(8,128)(2,1)S(1)} fusion(bf16[2,256,12,32]{1,3,2,0:T(8,128)(2,1)S(1)} %bitcast.208, f32[2,12,256,256]{2,3,1,0:T(8,128)} %fusion.140, f32[2,12,256,256]{2,3,1,0:T(8,128)} %get-tuple-element.183, f32[2,12,256]{2,1,0:T(8,128)S(1)} %get-tuple-element.184), kind=kOutput, calls=%fused_computation.29.clone.1 | convolution fusion | flops 111876352 | bytes 13393920 | tf_op jit(solution)/shard_map/while/body/eval_jaxpr/bhqk,bkhe->bqhe/dot_general | solution.py:165
  303.6 9.3 %fusion.141 = bf16[2,12,32,256]{3,2,1,0:T(8,128)(2,1)S(1)} fusion(bf16[2,256,12,32]{1,3,2,0:T(8,128)(2,1)S(1)} %bitcast.206, f32[2,12,256,256]{2,3,1,0:T(8,128)} %fusion.140, f32[2,12,256,256]{2,3,1,0:T(8,128)} %get-tuple-element.183, f32[2,12,256]{2,1,0:T(8,128)S(1)} %get-tuple-element.184), kind=kOutput, calls=%fused_computation.30.clone.1 | convolution fusion | flops 111876352 | bytes 13393920 | tf_op jit(solution)/shard_map/while/body/eval_jaxpr/bhqk,bqhe->bkhe/dot_general | solution.py:168
  312.9 3.8 fusion.139
  321.3 3.6 fusion.140
  324.9 4.9 fusion.138
  329.8 10.0 %fusion.142 = bf16[2,12,32,256]{3,2,1,0:T(8,128)(2,1)S(1)} fusion(bf16[2,256,12,32]{1,3,2,0:T(8,128)(2,1)S(1)} %bitcast.208, f32[2,12,256,256]{2,3,1,0:T(8,128)} %fusion.140, f32[2,12,256,256]{2,3,1,0:T(8,128)} %get-tuple-element.183, f32[2,12,256]{2,1,0:T(8,128)S(1)} %get-tuple-element.184), kind=kOutput, calls=%fused_computation.29.clone.1 | convolution fusion | flops 111876352 | bytes 13393920 | tf_op jit(solution)/shard_map/while/body/eval_jaxpr/bhqk,bkhe->bqhe/dot_general | solution.py:165
  339.8 9.3 %fusion.141 = bf16[2,12,32,256]{3,2,1,0:T(8,128)(2,1)S(1)} fusion(bf16[2,256,12,32]{1,3,2,0:T(8,128)(2,1)S(1)} %bitcast.206, f32[2,12,256,256]{2,3,1,0:T(8,128)} %fusion.140, f32[2,12,256,256]{2,3,1,0:T(8,128)} %get-tuple-element.183, f32[2,12,256]{2,1,0:T(8,128)S(1)} %get-tuple-element.184), kind=kOutput, calls=%fused_computation.30.clone.1 | convolution fusion | flops 111876352 | bytes 13393920 | tf_op jit(solution)/shard_map/while/body/eval_jaxpr/bhqk,bqhe->bkhe/dot_general | solution.py:168
  349.1 3.8 fusion.139
  355.0 6.3 %fusion.63 = f32[384,1152]{1,0:T(8,128)} fusion(bf16[2048,384]{1,0:T(8,128)(2,1)} %bitcast.233, bf16[2048,1152]{1,0:T(8,128)(2,1)} %bitcast.234), kind=kOutput, calls=%fused_computation.98 | convolution fusion | flops 1811939328 | bytes 8060928 | tf_op jit(solution)/shard_map/nd,nt->dt/dot_general | solution.py:227
  362.6 7.1 %add_convert_fusion.1 = bf16[2048,384]{1,0:T(8,128)(2,1)S(1)} fusion(f32[2048,384]{1,0:T(8,128)} %copy-done.8, bf16[2048,1536]{1,0:T(8,128)(2,1)} %copy-done.11, bf16[1536,384]{1,0:T(8,128)(2,1)S(1)} %copy-done.28), kind=kOutput, calls=%fused_computation.62 | convolution fusion | flops 2417491968 | bytes 12189696 | tf_op jit(solution)/shard_map/dot_general | solution.py:203
  369.7 2.4 copy.79
  372.1 3.7 reshape_reshape.52.source
  375.8 33.4 %shard_map.144 = bf16[128,16,384]{2,1,0:T(8,128)(2,1)S(1)} custom-call(bf16[128,16,384]{2,1,0:T(8,128)(2,1)S(1)} %reshape_reshape.52.source), custom_call_target="tpu_custom_call" | custom-call | tf_op jit(solution)/shard_map/pallas_call | solution.py:68
  410.3 3.6 reshape_reshape.53
  417.4 6.1 %multiply_reduce_fusion.4 = (f32[384]{0:T(512)S(1)}, f32[2048]{0:T(1024)S(1)}, f32[2048]{0:T(1024)S(1)}, f32[2048,384]{1,0:T(8,128)S(1)}) fusion(f32[8,16,4,2,2,1,384]{6,1,4,0,3,2,5:T(8,128)S(1)} %copy-done.7, f32[2048]{0:T(1024)S(1)} %copy-done.22, f32[2048]{0:T(1024)S(1)} %copy-done.20, f32[384]{0:T(512)S(1)} %copy-done.25, ...), kind=kOutput, calls=%fused_computation.56 | convolution fusion | flops 1818226304 | bytes 11930624 | tf_op jit(solution)/shard_map/nt,dt->nd/dot_general | solution.py:228
  425.2 2.4 copy.78
  427.6 3.7 reshape_reshape.60.source
  431.2 33.2 %shard_map.146 = bf16[128,16,384]{2,1,0:T(8,128)(2,1)S(1)} custom-call(bf16[128,16,384]{2,1,0:T(8,128)(2,1)S(1)} %reshape_reshape.60.source), custom_call_target="tpu_custom_call" | custom-call | tf_op jit(solution)/shard_map/pallas_call | solution.py:68
  465.6 3.5 reshape_reshape.61
  472.6 64.8 %all-reduce = (f32[384]{0:T(512)S(1)}, f32[384]{0:T(512)S(1)}) all-reduce(f32[384]{0:T(512)S(1)} %get-tuple-element.80, f32[384]{0:T(512)S(1)} %copy-done.26), channel_id=1, replica_groups=mesh['row'=8,'col'=16] {'row','col'}, use_global_device_ids=true, to_apply=%region_22.23 | all-reduce | flops 768 | bytes 6144 | tf_op jit(solution)/shard_map/psum | solution.py:307
  538.6 14.8 %all-reduce.4.cloned.1.call-done = (f32[384,1152]{1,0:T(8,128)}, f32[384,384]{1,0:T(8,128)}, f32[384,1536]{1,0:T(8,128)}, f32[1536,384]{1,0:T(8,128)}) async-done(((f32[384,1152]{1,0:T(8,128)}, f32[384,384]{1,0:T(8,128)}, f32[384,1536]{1,0:T(8,128)}, f32[1536,384]{1,0:T(8,128)}), (f32[384,1152]{1,0:T(8,128)}, f32[384,384]{1,0:T(8,128)}, f32[384,1536]{1,0:T(8,128)}, ...) | async-done | bytes 7077904 | tf_op jit(solution)/shard_map/psum | solution.py:307
  553.3 2.9 broadcast_multiply_fusion.2
  (139 shorter events, 62.3 us)
Async XLA Ops:
  7.2 170.8 %copy-start = (bf16[384,1536]{1,0:T(8,128)(2,1)S(1)}, bf16[384,1536]{1,0:T(8,128)(2,1)}, u32[]{:S(2)}) copy-start(bf16[384,1536]{1,0:T(8,128)(2,1)} %param.18) | copy-start | bytes 3538948
  7.2 546.2 %all-reduce.4.cloned.1.call-start = ((), (), s32[]{:S(2)}) async-start(), calls=%async_computation | async-start | bytes 14155776 | tf_op jit(solution)/shard_map/psum | solution.py:307
  53.8 1.1 copy-start.5
  64.4 5.1 copy-start.24
  66.8 50.6 %copy-start.19 = (f32[2048]{0:T(1024)}, f32[2048]{0:T(1024)S(1)}, u32[]{:S(2)}) copy-start(f32[2048]{0:T(1024)S(1)} %div.43) | copy-start | bytes 24580
  69.4 3.4 copy-start.16
  69.5 47.9 %copy-start.21 = (f32[2048]{0:T(1024)}, f32[2048]{0:T(1024)S(1)}, u32[]{:S(2)}) copy-start(f32[2048]{0:T(1024)S(1)} %rsqrt.21) | copy-start | bytes 24580
  111.0 1.1 copy-start.2
  115.9 2.5 copy-start.6
  118.3 1.2 copy-start.29
  130.5 43.1 %copy-start.17 = (bf16[384,384]{1,0:T(8,128)(2,1)S(1)}, bf16[384,384]{1,0:T(8,128)(2,1)}, u32[]{:S(2)}) copy-start(bf16[384,384]{1,0:T(8,128)(2,1)} %param.16) | copy-start | bytes 884740
  177.3 21.1 %copy-start.8 = (f32[2048,384]{1,0:T(8,128)}, f32[2048,384]{1,0:T(8,128)S(1)}, u32[]{:S(2)}) copy-start(f32[2048,384]{1,0:T(8,128)S(1)} %get-tuple-element.115) | copy-start | bytes 9437188
  177.3 0.8 copy-start.23
  178.0 4.4 copy-start.12
  178.0 4.4 copy-start.27
  182.4 22.1 %copy-start.11 = (bf16[2048,1536]{1,0:T(8,128)(2,1)}, bf16[2048,1536]{1,0:T(8,128)(2,1)S(1)}, u32[]{:S(2)}) copy-start(bf16[2048,1536]{1,0:T(8,128)(2,1)S(1)} %get-tuple-element.116) | copy-start | bytes 18874372
  198.4 2.0 copy-start.13
  200.4 4.1 copy-start.9
  361.3 1.3 copy-start.28
  409.1 1.1 copy-start.3
  414.3 3.0 copy-start.7
  414.3 3.0 copy-start.20
  414.3 3.0 copy-start.22
  414.3 3.0 copy-start.25
  414.3 3.0 copy-start.30
  417.4 6.1 %copy-start.10 = (f32[2048,384]{1,0:T(8,128)S(1)}, f32[2048,384]{1,0:T(8,128)}, u32[]{:S(2)}) copy-start(f32[2048,384]{1,0:T(8,128)} %copy-done.9) | copy-start | bytes 9437188
  464.5 1.1 copy-start.4
  469.6 3.0 copy-start.26
  553.3 3.0 copy-start.18
  553.3 3.8 copy-start.15
  556.3 2.5 copy-start.14
  557.2 3.1 copy-start.1
Sparse Core Ops, SparseCore 0:
  361.5 191.8 all-reduce.3

commit v2 on v0

v2 whole, which is shorter than its diff:
```python
import functools

import jax
import jax.numpy as jnp
from jax import lax
from jax.experimental import pallas as pl
from jax.experimental.pallas import tpu as pltpu
from jax.sharding import PartitionSpec as P

HEADS = 12
GRID = 16
GROUPS = 8
TOKENS = 256
D = 384
FF = 1536
WIDE = 32
CHUNK = 512

EPSILON = 1e-05
SQRT_HALF = 0.7071067811865476
INV_ROOT_TAU = 0.3989422804014327
LOG2E = 1.4426950408889634
SCORE_SCALE = WIDE ** (-0.5)
F32 = jnp.float32
BF16 = jnp.bfloat16


def dot_nn(a, b):
    return lax.dot_general(a, b, (((1,), (0,)), ((), ())), preferred_element_type=F32)


def dot_nt(a, b):
    return lax.dot_general(a, b, (((1,), (1,)), ((), ())), preferred_element_type=F32)


def dot_tn(a, b):
    return lax.dot_general(a, b, (((0,), (0,)), ((), ())), preferred_element_type=F32)


def mean0(values):
    return jnp.sum(values, axis=0, keepdims=True) * (1.0 / D)


def gelu_parts(pre):
    gauss = jnp.exp2(pre * pre * (-0.5 * LOG2E))
    t = 1.0 / (1.0 + (0.3275911 * SQRT_HALF) * jnp.abs(pre))
    poly = t * (0.127414796 + t * (-0.142248368 + t * (0.7107068705 + t * (-0.7265760135 + t * 0.5307027145))))
    tail = poly * gauss
    cdf = jnp.where(pre >= 0.0, 1.0 - tail, tail)
    return pre * cdf, cdf + pre * gauss * INV_ROOT_TAU


def spread(rows, values):
    for lane in range(D // 128):
        rows[lane] = values[:, lane * 128 : lane * 128 + 128].astype(F32)


def joined(rows):
    return jnp.concatenate([rows[lane] for lane in range(D // 128)], axis=1)


def take_group(rows, group):
    members = pl.ds(group, TOKENS, stride=GROUPS)
    return jnp.concatenate([rows[lane, members, :].T for lane in range(D // 128)], axis=0)


def put_group(rows, group, values):
    members = pl.ds(group, TOKENS, stride=GROUPS)
    for lane in range(D // 128):
        rows[lane, members, :] = values[lane * 128 : lane * 128 + 128].T


def project_group(group, x_rows, gain, joint_t, x_feat, triple, stats):
    values = take_group(x_rows, group)
    x_feat[group] = values.astype(BF16)
    center = values - mean0(values)
    inv = lax.rsqrt(mean0(center * center) + EPSILON)
    scaled = (center * inv * gain[...]).astype(BF16)
    triple[group] = dot_nn(joint_t[...], scaled).astype(BF16)


def attend_group(group, triple, mixed, stats):
    for head in range(HEADS):
        at = head * WIDE
        query = triple[group, at : at + WIDE]
        key = triple[group, D + at : D + at + WIDE]
        value = triple[group, 2 * D + at : 2 * D + at + WIDE]
        scores = dot_tn(key, query) * (SCORE_SCALE * LOG2E)
        top = jnp.max(scores, axis=0, keepdims=True)
        raised = jnp.exp2(scores - top)
        share = 1.0 / jnp.sum(raised, axis=0, keepdims=True)
        stats[group, 2 * head : 2 * head + 1] = top
        stats[group, 2 * head + 1 : 2 * head + 2] = share
        weights = (raised * share).astype(BF16)
        mixed[group, at : at + WIDE] = dot_nn(value, weights).astype(BF16)


def tail_group(
    group, x_feat, cot_rows, mixed, project, project_t, gain, expand, expand_t, reduce, reduce_t,
    result_rows, grad_att, grad_mixed, sum_project, sum_expand, sum_reduce, sum_gain,
):
    blend = mixed[group]
    cot32 = take_group(cot_rows, group)
    cot = cot32.astype(BF16)
    attended = x_feat[group].astype(F32) + dot_nn(project_t[...], blend)
    center = attended - mean0(attended)
    inv = lax.rsqrt(mean0(center * center) + EPSILON)
    normed = center * inv
    scaled = (normed * gain[...]).astype(BF16)
    result = attended
    grad_scaled = None
    for start in range(0, FF, CHUNK):
        part = slice(start, start + CHUNK)
        pre = dot_nn(expand_t[part, :], scaled)
        value, slope = gelu_parts(pre)
        hidden = value.astype(BF16)
        grad_hidden = dot_nn(reduce[part, :], cot).astype(BF16).astype(F32)
        grad_pre = (grad_hidden * slope).astype(BF16)
        result = result + dot_nn(reduce_t[:, part], hidden)
        back = dot_nn(expand[:, part], grad_pre)
        grad_scaled = back if grad_scaled is None else grad_scaled + back
        sum_reduce[part, :] += dot_nt(hidden, cot)
        sum_expand[part, :] += dot_nt(grad_pre, scaled)
    put_group(result_rows, group, result)
    sum_gain[...] += grad_scaled * normed
    lifted = grad_scaled * gain[...]
    grad = cot32 + inv * (lifted - mean0(lifted) - normed * mean0(lifted * normed))
    grad_att[group] = grad
    grad_b = grad.astype(BF16)
    sum_project[...] += dot_nt(blend, grad_b)
    grad_mixed[group] = dot_nn(project[...], grad_b).astype(BF16)


def attend_back_group(group, triple, stats, grad_mixed, grad_triple):
    for head in range(HEADS):
        at = head * WIDE
        query = triple[group, at : at + WIDE]
        key = triple[group, D + at : D + at + WIDE]
        value = triple[group, 2 * D + at : 2 * D + at + WIDE]
        grad_out = grad_mixed[group, at : at + WIDE]
        top = stats[group, 2 * head : 2 * head + 1]
        share = stats[group, 2 * head + 1 : 2 * head + 2]
        scores = dot_tn(key, query) * (SCORE_SCALE * LOG2E)
        weights = jnp.exp2(scores - top) * share
        grad_weights = dot_tn(value, grad_out)
        inner = jnp.sum(weights * grad_weights, axis=0, keepdims=True)
        grad_scores = (weights * (grad_weights - inner) * SCORE_SCALE).astype(BF16)
        grad_triple[at : at + WIDE] = dot_nn(key, grad_scores).astype(BF16)
        grad_triple[D + at : D + at + WIDE] = dot_nt(query, grad_scores).astype(BF16)
        grad_triple[2 * D + at : 2 * D + at + WIDE] = dot_nt(grad_out, weights.astype(BF16)).astype(BF16)


def head_back_group(group, x_feat, grad_att, grad_triple, gain, joint, grad_rows, sum_joint, sum_gain):
    values = x_feat[group].astype(F32)
    center = values - mean0(values)
    inv = lax.rsqrt(mean0(center * center) + EPSILON)
    normed = center * inv
    scaled = (normed * gain[...]).astype(BF16)
    sum_joint[...] += dot_nt(grad_triple[...], scaled)
    grad_scaled = dot_nn(joint[...], grad_triple[...])
    sum_gain[...] += grad_scaled * normed
    lifted = grad_scaled * gain[...]
    grad = grad_att[group] + inv * (lifted - mean0(lifted) - normed * mean0(lifted * normed))
    put_group(grad_rows, group, grad)


AXES = ("row", "col")
MESH = pl.DeviceIdType.MESH
POSITIONS = 262144
LANES = 128
BLOCK = 16
PIECE = 9
HALF = 8 * PIECE
SHARE = 2 * HALF
STRIDE = 32
ROWS = (D // LANES, GROUPS * TOKENS, LANES)
WHOLE = pl.BlockSpec(memory_space=pltpu.VMEM)


def shape(dims, dtype=BF16):
    return jax.ShapeDtypeStruct(dims, dtype)


def local_call(kernel, inputs, outs, scratch=(), flops=0, nbytes=0):
    single = not isinstance(outs, (list, tuple))
    count = 1 if single else len(outs)
    return pl.pallas_call(
        kernel,
        in_specs=[WHOLE] * len(inputs),
        out_specs=WHOLE if single else [WHOLE] * count,
        out_shape=outs,
        scratch_shapes=list(scratch),
        cost_estimate=pl.CostEstimate(flops=flops, bytes_accessed=nbytes, transcendentals=0),
        compiler_params=pltpu.CompilerParams(vmem_limit_bytes=56 * 2**20),
    )(*inputs)


def pack_kernel(tile, packed):
    def step(a, carry):
        near = tile[a].astype(F32)
        far = tile[STRIDE + a].astype(F32)
        for block in range(STRIDE // GROUPS):
            part = slice(block * GROUPS, block * GROUPS + GROUPS)
            packed[a * (STRIDE // GROUPS) + block] = jnp.concatenate([near[part], far[part]], axis=0).astype(BF16)
        return carry

    lax.fori_loop(0, STRIDE, step, 0, unroll=4)


def unpack_kernel(arrived, tile):
    def step(a, carry):
        blocks = [arrived[a * (STRIDE // GROUPS) + block].astype(F32) for block in range(STRIDE // GROUPS)]
        tile[a] = jnp.concatenate([b[:GROUPS] for b in blocks], axis=0).astype(BF16)
        tile[STRIDE + a] = jnp.concatenate([b[GROUPS:] for b in blocks], axis=0).astype(BF16)
        return carry

    lax.fori_loop(0, STRIDE, step, 0, unroll=4)


def front_kernel(arrived, gain, joint_t, x_feat, triple, mixed, stats, rows):
    spread(rows, arrived)

    def step(group, carry):
        project_group(group, rows, gain, joint_t, x_feat, triple, stats)
        attend_group(group, triple, mixed, stats)
        return carry

    lax.fori_loop(0, GROUPS, step, 0)


def middle_kernel(
    x_feat, cot, mixed, project, project_t, gain, expand, expand_t, reduce, reduce_t,
    result, grad_att, grad_mixed, grad_project, grad_expand, grad_reduce, grad_gain,
    cot_rows, result_rows, sum_project, sum_expand, sum_reduce, sum_gain,
):
    spread(cot_rows, cot)
    for total in (sum_project, sum_expand, sum_reduce, sum_gain):
        total[...] = jnp.zeros_like(total)

    def step(group, carry):
        tail_group(
            group, x_feat, cot_rows, mixed, project, project_t, gain, expand, expand_t, reduce, reduce_t,
            result_rows, grad_att, grad_mixed, sum_project, sum_expand, sum_reduce, sum_gain,
        )
        return carry

    lax.fori_loop(0, GROUPS, step, 0)
    result[...] = joined(result_rows).astype(BF16)
    for out, total in ((grad_project, sum_project), (grad_expand, sum_expand), (grad_reduce, sum_reduce)):
        out[...] = total[...].astype(BF16)
    grad_gain[...] = jnp.sum(sum_gain[...].T, axis=0, keepdims=True)


def back_kernel(
    x_feat, triple, stats, grad_mixed, grad_att, gain, joint,
    grad_in, grad_joint, grad_gain,
    grad_triple, grad_rows, sum_joint, sum_gain,
):
    for total in (sum_joint, sum_gain):
        total[...] = jnp.zeros_like(total)

    def step(group, carry):
        attend_back_group(group, triple, stats, grad_mixed, grad_triple)
        head_back_group(group, x_feat, grad_att, grad_triple, gain, joint, grad_rows, sum_joint, sum_gain)
        return carry

    lax.fori_loop(0, GROUPS, step, 0)
    grad_in[...] = joined(grad_rows).astype(BF16)
    grad_joint[...] = sum_joint[...].astype(BF16)
    grad_gain[...] = jnp.sum(sum_gain[...].T, axis=0, keepdims=True)


def total_kernel(
    expand, reduce, joint, project, gains,
    total, gain_total,
    mine, sibling, own, in_a, part, in_b, gain_pair, gain_a, gain_b,
    pair_sems, a_sems, b_sems, gather_sems, last_sems, gain_sems,
):
    row, col = lax.axis_index("row"), lax.axis_index("col")
    core = lax.rem(col, 2)
    place = col // 2
    other = (row, col + 1 - 2 * core)
    slots = (place, row)

    def peer(half, index):
        return (row, index * 2 + core) if half == 0 else (index, col)

    barrier = pltpu.get_barrier_semaphore()
    pl.semaphore_signal(barrier, inc=1, device_id=other, device_id_type=MESH)
    for half in range(2):
        for step in range(1, 8):
            index = lax.rem(slots[half] + step, 8)
            pl.semaphore_signal(barrier, inc=1, device_id=peer(half, index), device_id_type=MESH)

    for side in range(2):
        at = side * SHARE
        for source in (expand, reduce, joint, project):
            blocks = source.shape[0] // 2
            mine[at : at + blocks] = source[side * blocks : side * blocks + blocks]
            at += blocks
    gain_pair[0] = gains[...]
    pl.semaphore_wait(barrier, 15)

    def copy(source, target, sems, index, device):
        return pltpu.make_async_remote_copy(
            src_ref=source, dst_ref=target, send_sem=sems.at[0, index], recv_sem=sems.at[1, index],
            device_id=device, device_id_type=MESH,
        )

    def settle(sent, landed, sems, index):
        pltpu.make_async_copy(sent, sent, sems.at[0, index]).wait()
        pltpu.make_async_copy(landed, landed, sems.at[1, index]).wait()

    def start_all(source, target, sems, index, half):
        def step(offset, carry):
            q = lax.rem(slots[half] + offset, 8)
            copy(source(q), target, sems, index, peer(half, q)).start()
            return carry

        lax.fori_loop(1, 8, step, 0)

    away = (1 - core) * SHARE
    here = core * SHARE
    pair = [
        copy(mine.at[pl.ds(away + half * HALF, HALF)], sibling.at[half], pair_sems, half, other) for half in range(2)
    ]
    gain_first = copy(gain_pair.at[0], gain_pair.at[1], gain_sems, 0, other)
    for one in pair:
        one.start()
    gain_first.start()
    for half in range(2):
        pair[half].wait()

        def add(q, carry):
            kept = mine[pl.ds(here + half * HALF + q * PIECE, PIECE)].astype(F32)
            own[half, q] = (kept + sibling[half, pl.ds(q * PIECE, PIECE)].astype(F32)).astype(BF16)
            return carry

        lax.fori_loop(0, 8, add, 0)
        start_all(lambda q: own.at[half, q], in_a.at[half, slots[half]], a_sems, half, half)
        in_a[half, slots[half]] = own[half, slots[half]]
    gain_first.wait()
    gain_a[place] = gain_pair[0] + gain_pair[1]
    start_all(lambda q: gain_a.at[place], gain_a.at[place], gain_sems, 1, 0)

    def summed(pieces):
        acc = pieces[0].astype(F32)
        for q in range(1, 8):
            acc = acc + pieces[q].astype(F32)
        return acc

    for half in range(2):
        settle(own.at[half, pl.ds(0, 7)], in_a.at[half, pl.ds(0, 7)], a_sems, half)

        def add(block, carry):
            part[half, block] = summed([in_a[half, q, block] for q in range(8)]).astype(BF16)
            return carry

        lax.fori_loop(0, PIECE, add, 0)
        start_all(lambda q: part.at[half], in_b.at[half, slots[1 - half]], b_sems, half, 1 - half)
        in_b[half, slots[1 - half]] = part[half]
    settle(gain_a.at[pl.ds(0, 7)], gain_a.at[pl.ds(0, 7)], gain_sems, 1)
    gain_b[row] = summed([gain_a[q] for q in range(8)])
    start_all(lambda q: gain_b.at[row], gain_b.at[row], gain_sems, 2, 1)

    for half in range(2):
        settle(in_b.at[half, pl.ds(0, 7)], in_b.at[half, pl.ds(0, 7)], b_sems, half)
        base = here + half * HALF + slots[half] * PIECE

        def add(block, carry):
            total[base + block] = summed([in_b[half, q, block] for q in range(8)]).astype(BF16)
            return carry

        lax.fori_loop(0, PIECE, add, 0)
        spot = total.at[pl.ds(base, PIECE)]
        start_all(lambda q: spot, spot, gather_sems, half, half)
    settle(gain_b.at[pl.ds(0, 7)], gain_b.at[pl.ds(0, 7)], gain_sems, 2)
    gain_total[...] = summed([gain_b[q] for q in range(8)])

    last = []
    for half in range(2):
        seven = total.at[pl.ds(0, 7 * PIECE)]
        settle(seven, seven, gather_sems, half)
        spot = total.at[pl.ds(here + half * HALF, HALF)]
        last.append(copy(spot, spot, last_sems, half, other))
        last[-1].start()
    for one in last:
        one.wait()


def sum_over_devices(expand, reduce, joint, project, gains):
    dma = pltpu.SemaphoreType.DMA
    piece = (PIECE, BLOCK, D)
    return pl.pallas_call(
        total_kernel,
        in_specs=[WHOLE] * 5,
        out_specs=[WHOLE] * 2,
        out_shape=[shape((2 * SHARE, BLOCK, D)), shape((8, D), F32)],
        scratch_shapes=[
            pltpu.VMEM((2 * SHARE, BLOCK, D), BF16),
            pltpu.VMEM((2, HALF, BLOCK, D), BF16),
            pltpu.VMEM((2, 8) + piece, BF16),
            pltpu.VMEM((2, 8) + piece, BF16),
            pltpu.VMEM((2,) + piece, BF16),
            pltpu.VMEM((2, 8) + piece, BF16),
            pltpu.VMEM((2, 8, D), F32),
            pltpu.VMEM((8, 8, D), F32),
            pltpu.VMEM((8, 8, D), F32),
            dma((2, 2)), dma((2, 2)), dma((2, 2)), dma((2, 2)), dma((2, 2)), dma((2, 3)),
        ],
        cost_estimate=pl.CostEstimate(flops=10**9, bytes_accessed=10**8, transcendentals=0),
        compiler_params=pltpu.CompilerParams(
            collective_id=0, has_side_effects=True, vmem_limit_bytes=48 * 2**20
        ),
    )(*[g.reshape(-1, BLOCK, D) for g in (expand, reduce, joint, project)], gains)


def swap(blocks):
    return lax.all_to_all(blocks, AXES, split_axis=0, concat_axis=0, tiled=True)


def shards(
    activations, cotangent, first_gain, joint_weight, output_weight, second_gain, expand_weight, reduce_weight
):
    devices = lax.axis_size("row") * lax.axis_size("col")
    blocks = (devices, BLOCK, D)
    rows = (devices * BLOCK, D)
    feat = (GROUPS, D, TOKENS)
    gain_a = first_gain[:, None]
    gain_b = second_gain[:, None]

    act = swap(local_call(pack_kernel, [activations], shape(blocks))).reshape(rows)
    cot = swap(local_call(pack_kernel, [cotangent], shape(blocks))).reshape(rows)
    x_feat, triple, mixed, stats = local_call(
        front_kernel,
        [act, gain_a, joint_weight.T],
        [shape(feat), shape((GROUPS, 3 * D, TOKENS)), shape(feat), shape((GROUPS, 2 * HEADS, TOKENS), F32)],
        [pltpu.VMEM(ROWS, F32)],
        flops=4 * 10**10, nbytes=10**7,
    )
    result, grad_att, grad_mixed, part_project, part_expand, part_reduce, part_second = local_call(
        middle_kernel,
        [
            x_feat, cot, mixed, output_weight, output_weight.T, gain_b,
            expand_weight, expand_weight.T, reduce_weight, reduce_weight.T,
        ],
        [
            shape(rows), shape(feat, F32), shape(feat),
            shape((D, D)), shape((FF, D)), shape((FF, D)), shape((1, D), F32),
        ],
        [
            pltpu.VMEM(ROWS, F32), pltpu.VMEM(ROWS, F32),
            pltpu.VMEM((D, D), F32), pltpu.VMEM((FF, D), F32), pltpu.VMEM((FF, D), F32), pltpu.VMEM((D, TOKENS), F32),
        ],
        flops=4 * 10**10, nbytes=10**7,
    )
    block_out = swap(result.reshape(blocks))
    grad_in, part_joint, part_first = local_call(
        back_kernel,
        [x_feat, triple, stats, grad_mixed, grad_att, gain_a, joint_weight],
        [shape(rows), shape((3 * D, D)), shape((1, D), F32)],
        [
            pltpu.VMEM((3 * D, TOKENS), BF16), pltpu.VMEM(ROWS, F32),
            pltpu.VMEM((3 * D, D), F32), pltpu.VMEM((D, TOKENS), F32),
        ],
        flops=4 * 10**10, nbytes=10**7,
    )
    grad_in = swap(grad_in.reshape(blocks))
    gains = jnp.concatenate([part_first, part_second, jnp.zeros((6, D), F32)], axis=0)
    total, gain_total = sum_over_devices(part_expand, part_reduce, part_joint, part_project, gains)
    tile = activations.shape
    block_out = local_call(unpack_kernel, [block_out], shape(tile))
    grad_in = local_call(unpack_kernel, [grad_in], shape(tile))

    factor = float(POSITIONS) ** -0.5
    sides = total.reshape(2, SHARE * BLOCK, D)

    def cut(start, size):
        return sides[:, start : start + size].reshape(2 * size, D).astype(F32) * factor

    half = FF // 2
    grad_expand = cut(0, half).T
    grad_reduce = cut(half, half)
    grad_joint = cut(FF, 3 * D // 2).T
    grad_project = cut(FF + 3 * D // 2, D // 2)
    return (
        block_out, grad_in, grad_joint, grad_project, grad_expand, grad_reduce,
        gain_total[0] * factor, gain_total[1] * factor,
    )


def solution(mesh):
    tile = P("row", "col", None)
    return jax.shard_map(
        shards,
        mesh=mesh,
        in_specs=(tile, tile) + (P(),) * 6,
        out_specs=(tile, tile) + (P(),) * 6,
        check_vma=False,
    )
```

time: 529 us -> 318 us (0.60); the launches traced: 519 us -> 315 us
  Pallas kernels: 0 us -> 222 us
  matrix products: 218 us -> 0 us
  waiting for transfers between devices: 86.5 us -> 14.1 us
  local copies, waits for them, and re-layouts: 70.6 us -> 13.9 us
  blocking collectives: 78.1 us -> 34.6 us
  other arithmetic: 22.4 us -> 7.12 us
  between operations: 15 us -> 0.73 us
  starting transfers between devices: 27.6 us -> 22.1 us
    pallas_call x0 -> x8, Pallas kernels: none -> 222 us  [the longest x7 139 us: local_call(): pl.pallas_call(kernel, in_specs=[WHOLE] * len(inputs), out_specs=WHOLE if...]
    dot_general x32 -> x0, matrix products: 179 us -> none  [the longest x4 40.1 us: attend_backward(): jnp.einsum('bhqk,bkhe->bqhe', grad_scores, key_rows, preferred_element_ty...]
    psum x1 -> x0, blocking collectives: 78.1 us -> none  [shards(): lax.psum((grad_joint, grad_out, grad_up, grad_down, grad_first, grad_seco...]
    psum x1 -> x0, waiting for transfers between devices: 40.8 us -> none  [shards(): lax.psum((grad_joint, grad_out, grad_up, grad_down, grad_first, grad_seco...]
    sub x8 -> x0, matrix products: 39 us -> none  [attend(): weights = jnp.exp(scores - row_max)]
    all_to_all x0 -> x1, blocking collectives: none -> 34.6 us  [swap(): return lax.all_to_all(blocks, AXES, split_axis=0, concat_axis=0, tiled=True)]
    all_to_all x4 -> x3, waiting for transfers between devices: 45.7 us -> 14.1 us  [swap(): return lax.all_to_all(blocks, AXES, split_axis=0, concat_axis=0, tiled=True)]
    reshape x6 -> x0, local copies, waits for them, and re-layouts: 17.2 us -> none  [the longest x4 11 us: exchange_both(): blocks = blocks.reshape(-1, *inside)]
  transfers between devices with their start and end apart: 5 -> 3, of which waited for: 4 -> 1; matrix products, arithmetic and copies ran while one was open for 10% -> 6% of each run, Pallas kernels for 0% -> 41%
where the time goes in v2:
time: 318 us; the launch traced here: 315 us
  Pallas kernels  222 us (70%)
  blocking collectives  34.6 us (11%)
  starting transfers between devices  22.1 us (7%)
  waiting for transfers between devices  14.1 us (4%)
  local copies, waits for them, and re-layouts  13.9 us (4%)
  other arithmetic  7.12 us (2%)
    pallas_call x7, Pallas kernels, local_call(): pl.pallas_call(kernel, in_specs=[WHOLE] * len(inputs), out_specs=WHOLE if...  139 us
    pallas_call x1, Pallas kernels, sum_over_devices(): pl.pallas_call(total_kernel, in_specs=[WHOLE] * 5, out_specs=[WHOLE] * 2,...  83.4 us
    all_to_all x1, blocking collectives, swap(): return lax.all_to_all(blocks, AXES, split_axis=0, concat_axis=0, tiled=True)  34.6 us
    all_to_all x3, starting transfers between devices, swap(): return lax.all_to_all(blocks, AXES, split_axis=0, concat_axis=0, tiled=True)  22.1 us
    all_to_all x3, waiting for transfers between devices, swap(): return lax.all_to_all(blocks, AXES, split_axis=0, concat_axis=0, tiled=True)  14.1 us
    unnamed x31, local copies, waits for them, and re-layouts  10.3 us
    mul x3, other arithmetic, cut(): sides[:, start:start + size].reshape(2 * size, D).astype(F32) * factor  6.44 us
  transfers between devices with their start and end apart: 3, of which 1 were waited for; matrix products, arithmetic and copies ran while one was open for 6% of the time, Pallas kernels for 41%

profile of v2, /device:TPU:1, one launch (start us, length us, event | category | flops | bytes accessed | tf_op | source)
XLA Modules:
  0.0 314.6 jit_solution(13637969070025468235)
XLA Ops:
  0.6 2.7 shard_map.143
  3.4 0.0 copy-start.9
  3.4 0.0 copy-start.7
  3.4 11.5 %all-to-all-start = ((bf16[128,16,384]{2,1,0:T(8,128)(2,1)}), bf16[128,16,384]{2,1,0:T(8,128)(2,1)S(1)}, u32[]{:S(2)}, u32[]{:S(2)}) async-start(bf16[128,16,384]{2,1,0:T(8,128)(2,1)} %shard_map.143), calls=%async_computation | async-start | bytes 3145728 | tf_op jit(solution)/shard_map/all_to_all | solution.py:419
  14.9 0.0 copy-done.9
  14.9 0.8 broadcast_in_dim.12.gain
  15.7 0.0 copy-done.7
  15.7 1.3 copy.22
  17.0 0.0 copy-start.6
  17.0 2.8 shard_map.145
  19.8 0.0 copy-done.6
  19.8 1.4 copy.25
  21.2 0.0 copy-start.8
  21.2 0.0 copy-start.10
  21.2 2.4 copy.26
  23.7 0.0 copy-done.8
  23.7 0.9 copy.24
  24.6 0.0 copy-done.10
  24.6 0.8 broadcast_in_dim.13.gain
  25.4 14.1 %all-to-all-done = bf16[128,16,384]{2,1,0:T(8,128)(2,1)S(1)} async-done(((bf16[128,16,384]{2,1,0:T(8,128)(2,1)}), bf16[128,16,384]{2,1,0:T(8,128)(2,1)S(1)}, u32[]{:S(2)}, u32[]{:S(2)}) %all-to-all-start) | async-done | bytes 1572896 | tf_op jit(solution)/shard_map/all_to_all | solution.py:419
  39.4 0.0 copy-start.5
  39.4 1.1 copy-done.5
  40.6 4.7 %all-to-all-start.1 = ((bf16[128,16,384]{2,1,0:T(8,128)(2,1)}), bf16[128,16,384]{2,1,0:T(8,128)(2,1)S(1)}, u32[]{:S(2)}, u32[]{:S(2)}) async-start(bf16[128,16,384]{2,1,0:T(8,128)(2,1)} %shard_map.145), calls=%async_computation.1 | async-start | bytes 3145728 | tf_op jit(solution)/shard_map/all_to_all | solution.py:419
  45.3 40.4 %shard_map.144 = (bf16[8,384,256]{2,1,0:T(8,128)(2,1)}, bf16[8,1152,256]{2,1,0:T(8,128)(2,1)}, bf16[8,384,256]{2,1,0:T(8,128)(2,1)}, f32[8,24,256]{2,1,0:T(8,128)}) custom-call(bf16[2048,384]{1,0:T(8,128)(2,1)} %bitcast.33, f32[384,1]{1,0:T(8,128)} %broadcast_in_dim.12.gain, bf16[1152,384]{1,0:T(8,128)(2,1)} %bitcast.37), custom_call_target="tpu_custom_call" | custom-call | flops 40000000000 | bytes 10000000 | tf_op jit(solution)/shard_map/pallas_call | solution.py:187
  85.6 0.0 all-to-all-done.1
  85.6 0.0 copy-start.4
  85.6 1.1 copy-done.4
  86.8 41.4 %shard_map.146 = (bf16[2048,384]{1,0:T(8,128)(2,1)}, f32[8,384,256]{2,1,0:T(8,128)}, bf16[8,384,256]{2,1,0:T(8,128)(2,1)}, bf16[384,384]{1,0:T(8,128)(2,1)}, bf1...) custom-call(bf16[8,384,256]{2,1,0:T(8,128)(2,1)} %get-tuple-element.24.x_feat, ...), custom_call_target="tpu_custom_call" | custom-call | flops 40000000000 | bytes 10000000 | tf_op jit(solution)/shard_map/pallas_call | solution.py:187
  128.2 46.1 %shard_map.148 = (bf16[2048,384]{1,0:T(8,128)(2,1)}, bf16[1152,384]{1,0:T(8,128)(2,1)}, f32[1,384]{1,0:T(1,128)}) custom-call(bf16[8,384,256]{2,1,0:T(8,128)(2,1)} %get-tuple-element.24.x_feat, bf16[8,1152,256]{2,1,0:T(8,128)(2,1)} %get-tuple-element.27.triple, f32[8,24,256]{2,1,0:T(8,128)} %get-tuple-element.28.stats, ...), custom_call_target="tpu_custom_call" | custom-call | flops 40000000000 | bytes 10000000 | tf_op jit(solution)/shard_map/pallas_call | solution.py:187
  174.3 0.0 copy-start.2
  174.3 34.6 %all_to_all.20.arrived = bf16[128,16,384]{2,1,0:T(8,128)(2,1)} all-to-all(bf16[128,16,384]{2,1,0:T(8,128)(2,1)} %bitcast.34), channel_id=1, replica_groups=mesh['row'=8,'col'=16] {'row','col'}, dimensions={0} | all-to-all | bytes 3145728 | tf_op jit(solution)/shard_map/all_to_all | solution.py:419
  208.9 0.0 copy-start.11
  208.9 0.0 copy-start.12
  208.9 0.0 copy-start
  208.9 0.0 copy-start.1
  208.9 0.0 copy-start.3
  208.9 5.9 %all-to-all-start.2 = ((bf16[128,16,384]{2,1,0:T(8,128)(2,1)}), bf16[128,16,384]{2,1,0:T(8,128)(2,1)}, u32[]{:S(2)}, u32[]{:S(2)}) async-start(bf16[128,16,384]{2,1,0:T(8,128)(2,1)} %bitcast.31), calls=%async_computation.2 | async-start | bytes 3145728 | tf_op jit(solution)/shard_map/all_to_all | solution.py:419
  214.8 0.1 pad.2.clone
  214.8 0.0 copy-done.11
  214.8 0.0 copy-done.12
  214.8 0.1 maximum_maximum_fusion.gains
  214.9 0.0 copy-done.2
  214.9 0.0 copy-done
  214.9 0.0 copy-done.1
  214.9 0.0 copy-done.3
  214.9 83.4 %shard_map.150 = (bf16[288,16,384]{2,1,0:T(8,128)(2,1)}, f32[8,384]{1,0:T(8,128)S(1)}) custom-call(bf16[96,16,384]{2,1,0:T(8,128)(2,1)S(1)} %bitcast.20, bf16[96,16,384]{2,1,0:T(8,128)(2,1)S(1)} %bitcast.21, bf16[72,16,384]{2,1,0:T(8,128)(2,1)S(1)} %bitcast.22, bf16[24,16,384]{2,1,0:T(8,128)(2,1)S(1)} %bitcast.23, f32[8,384]{1,0:T(8,128)S(1)} %maximum_maximum_fusion.gains), custom_call_target="tpu_custom_call" | custom-call | flops 1000000000 | bytes 100000000 | tf_op jit(solution)/shard_map/pallas_call | solution.py:394
  298.3 3.3 %convert_multiply_fusion = (f32[2,768,384]{2,1,0:T(8,128)}, f32[2,768,384]{2,1,0:T(8,128)S(1)}) fusion(bf16[2,2304,384]{2,1,0:T(8,128)(2,1)} %bitcast.26), kind=kLoop, calls=%fused_computation | loop fusion | flops 2359296 | bytes 7077888 | tf_op jit(solution)/shard_map/mul | solution.py:479
  301.7 1.9 copy.29
  303.6 1.3 convert_multiply_fusion.2
  304.9 1.9 copy.30
  306.8 0.6 multiply_reduce_fusion
  307.4 1.8 convert_multiply_fusion.3
  309.2 2.7 shard_map.149
  311.9 0.0 all-to-all-done.2.arrived
  311.9 2.7 shard_map.147
  (1 shorter events, 0.0 us)
Async XLA Ops:
  3.4 11.5 %copy-start.9 = (f32[384]{0:T(512)S(1)}, f32[384]{0:T(512)}, u32[]{:S(2)}) copy-start(f32[384]{0:T(512)} %param.10) | copy-start | bytes 4612
  3.4 12.3 %copy-start.7 = (bf16[384,1152]{1,0:T(8,128)(2,1)S(1)}, bf16[384,1152]{1,0:T(8,128)(2,1)}, u32[]{:S(2)}) copy-start(bf16[384,1152]{1,0:T(8,128)(2,1)} %joint.1) | copy-start | bytes 2654212
  3.4 36.1 %all-to-all-start = ((bf16[128,16,384]{2,1,0:T(8,128)(2,1)}), bf16[128,16,384]{2,1,0:T(8,128)(2,1)S(1)}, u32[]{:S(2)}, u32[]{:S(2)}) async-start(bf16[128,16,384]{2,1,0:T(8,128)(2,1)} %shard_map.143), calls=%async_computation | async-start | bytes 3145728 | tf_op jit(solution)/shard_map/all_to_all | solution.py:419
  17.0 2.8 copy-start.6
  21.2 2.5 copy-start.8
  21.2 3.4 %copy-start.10 = (f32[384]{0:T(512)S(1)}, f32[384]{0:T(512)}, u32[]{:S(2)}) copy-start(f32[384]{0:T(512)} %param.13) | copy-start | bytes 4612
  39.4 1.1 copy-start.5
  40.6 45.1 %all-to-all-start.1 = ((bf16[128,16,384]{2,1,0:T(8,128)(2,1)}), bf16[128,16,384]{2,1,0:T(8,128)(2,1)S(1)}, u32[]{:S(2)}, u32[]{:S(2)}) async-start(bf16[128,16,384]{2,1,0:T(8,128)(2,1)} %shard_map.145), calls=%async_computation.1 | async-start | bytes 3145728 | tf_op jit(solution)/shard_map/all_to_all | solution.py:419
  85.6 1.1 copy-start.4
  174.3 40.6 %copy-start.2 = (bf16[1152,384]{1,0:T(8,128)(2,1)S(1)}, bf16[1152,384]{1,0:T(8,128)(2,1)}, u32[]{:S(2)}) copy-start(bf16[1152,384]{1,0:T(8,128)(2,1)} %get-tuple-element.34) | copy-start | bytes 2654212
  208.9 6.0 %copy-start.11 = (f32[1,384]{1,0:T(1,128)S(1)}, f32[1,384]{1,0:T(1,128)}, u32[]{:S(2)}) copy-start(f32[1,384]{1,0:T(1,128)} %get-tuple-element.37) | copy-start | bytes 4612
  208.9 6.0 %copy-start.12 = (f32[1,384]{1,0:T(1,128)S(1)}, f32[1,384]{1,0:T(1,128)}, u32[]{:S(2)}) copy-start(f32[1,384]{1,0:T(1,128)} %get-tuple-element.36) | copy-start | bytes 4612
  208.9 6.1 %copy-start = (bf16[1536,384]{1,0:T(8,128)(2,1)S(1)}, bf16[1536,384]{1,0:T(8,128)(2,1)}, u32[]{:S(2)}) copy-start(bf16[1536,384]{1,0:T(8,128)(2,1)} %get-tuple-element.32) | copy-start | bytes 3538948
  208.9 6.1 %copy-start.1 = (bf16[1536,384]{1,0:T(8,128)(2,1)S(1)}, bf16[1536,384]{1,0:T(8,128)(2,1)}, u32[]{:S(2)}) copy-start(bf16[1536,384]{1,0:T(8,128)(2,1)} %get-tuple-element.33) | copy-start | bytes 3538948
  208.9 6.1 %copy-start.3 = (bf16[384,384]{1,0:T(8,128)(2,1)S(1)}, bf16[384,384]{1,0:T(8,128)(2,1)}, u32[]{:S(2)}) copy-start(bf16[384,384]{1,0:T(8,128)(2,1)} %get-tuple-element.35) | copy-start | bytes 884740
  208.9 103.0 %all-to-all-start.2 = ((bf16[128,16,384]{2,1,0:T(8,128)(2,1)}), bf16[128,16,384]{2,1,0:T(8,128)(2,1)}, u32[]{:S(2)}, u32[]{:S(2)}) async-start(bf16[128,16,384]{2,1,0:T(8,128)(2,1)} %bitcast.31), calls=%async_computation.2 | async-start | bytes 3145728 | tf_op jit(solution)/shard_map/all_to_all | solution.py:419

commit v3 on v2

v3 whole, which is shorter than its diff:
```python
import jax
import jax.numpy as jnp
from jax import lax
from jax.experimental import pallas as pl
from jax.experimental.pallas import tpu as pltpu
from jax.sharding import PartitionSpec as P

HEADS = 12
GRID = 16
GROUPS = 8
TOKENS = 256
D = 384
FF = 1536
WIDE = 32
CHUNK = 512

EPSILON = 1e-05
SQRT_HALF = 0.7071067811865476
INV_ROOT_TAU = 0.3989422804014327
LOG2E = 1.4426950408889634
SCORE_SCALE = WIDE ** (-0.5)
F32 = jnp.float32
BF16 = jnp.bfloat16


def dot_nn(a, b):
    return lax.dot_general(a, b, (((1,), (0,)), ((), ())), preferred_element_type=F32)


def dot_nt(a, b):
    return lax.dot_general(a, b, (((1,), (1,)), ((), ())), preferred_element_type=F32)


def dot_tn(a, b):
    return lax.dot_general(a, b, (((0,), (0,)), ((), ())), preferred_element_type=F32)


def mean0(values):
    return jnp.sum(values, axis=0, keepdims=True) * (1.0 / D)


def gelu_parts(pre):
    gauss = jnp.exp2(pre * pre * (-0.5 * LOG2E))
    t = 1.0 / (1.0 + (0.3275911 * SQRT_HALF) * jnp.abs(pre))
    poly = t * (0.127414796 + t * (-0.142248368 + t * (0.7107068705 + t * (-0.7265760135 + t * 0.5307027145))))
    tail = poly * gauss
    cdf = jnp.where(pre >= 0.0, 1.0 - tail, tail)
    return pre * cdf, cdf + pre * gauss * INV_ROOT_TAU


def take_group(rows, group):
    members = pl.ds(group, TOKENS, stride=GROUPS)
    return jnp.concatenate([rows[lane, members, :].T for lane in range(D // 128)], axis=0)


def put_group(rows, group, values):
    members = pl.ds(group, TOKENS, stride=GROUPS)
    for lane in range(D // 128):
        rows[lane, members, :] = values[lane * 128 : lane * 128 + 128].T


def project_group(group, x_rows, gain, joint_t, x_feat, triple, stats):
    values = take_group(x_rows, group)
    x_feat[group] = values.astype(BF16)
    center = values - mean0(values)
    inv = lax.rsqrt(mean0(center * center) + EPSILON)
    scaled = (center * inv * gain[...]).astype(BF16)
    triple[group] = dot_nn(joint_t[...], scaled).astype(BF16)


def attend_group(group, triple, mixed, stats):
    for head in range(HEADS):
        at = head * WIDE
        query = triple[group, at : at + WIDE]
        key = triple[group, D + at : D + at + WIDE]
        value = triple[group, 2 * D + at : 2 * D + at + WIDE]
        scores = dot_tn(key, query) * (SCORE_SCALE * LOG2E)
        top = jnp.max(scores, axis=0, keepdims=True)
        raised = jnp.exp2(scores - top)
        share = 1.0 / jnp.sum(raised, axis=0, keepdims=True)
        stats[group, 2 * head : 2 * head + 1] = top
        stats[group, 2 * head + 1 : 2 * head + 2] = share
        weights = (raised * share).astype(BF16)
        mixed[group, at : at + WIDE] = dot_nn(value, weights).astype(BF16)


def tail_group(
    group, x_feat, cot_rows, mixed, project, project_t, gain, expand, expand_t, reduce, reduce_t,
    result_rows, grad_att, grad_mixed, sum_project, sum_expand, sum_reduce, sum_gain,
):
    blend = mixed[group]
    cot32 = take_group(cot_rows, group)
    cot = cot32.astype(BF16)
    attended = x_feat[group].astype(F32) + dot_nn(project_t[...], blend)
    center = attended - mean0(attended)
    inv = lax.rsqrt(mean0(center * center) + EPSILON)
    normed = center * inv
    scaled = (normed * gain[...]).astype(BF16)
    result = attended
    grad_scaled = None
    for start in range(0, FF, CHUNK):
        part = slice(start, start + CHUNK)
        pre = dot_nn(expand_t[part, :], scaled)
        value, slope = gelu_parts(pre)
        hidden = value.astype(BF16)
        grad_hidden = dot_nn(reduce[part, :], cot).astype(BF16).astype(F32)
        grad_pre = (grad_hidden * slope).astype(BF16)
        result = result + dot_nn(reduce_t[:, part], hidden)
        back = dot_nn(expand[:, part], grad_pre)
        grad_scaled = back if grad_scaled is None else grad_scaled + back
        sum_reduce[part, :] += dot_nt(hidden, cot)
        sum_expand[part, :] += dot_nt(grad_pre, scaled)
    put_group(result_rows, group, result)
    sum_gain[...] += grad_scaled * normed
    lifted = grad_scaled * gain[...]
    grad = cot32 + inv * (lifted - mean0(lifted) - normed * mean0(lifted * normed))
    grad_att[group] = grad
    grad_b = grad.astype(BF16)
    sum_project[...] += dot_nt(blend, grad_b)
    grad_mixed[group] = dot_nn(project[...], grad_b).astype(BF16)


def attend_back_group(group, triple, stats, grad_mixed, grad_triple):
    for head in range(HEADS):
        at = head * WIDE
        query = triple[group, at : at + WIDE]
        key = triple[group, D + at : D + at + WIDE]
        value = triple[group, 2 * D + at : 2 * D + at + WIDE]
        grad_out = grad_mixed[group, at : at + WIDE]
        top = stats[group, 2 * head : 2 * head + 1]
        share = stats[group, 2 * head + 1 : 2 * head + 2]
        scores = dot_tn(key, query) * (SCORE_SCALE * LOG2E)
        weights = jnp.exp2(scores - top) * share
        grad_weights = dot_tn(value, grad_out)
        inner = jnp.sum(weights * grad_weights, axis=0, keepdims=True)
        grad_scores = (weights * (grad_weights - inner) * SCORE_SCALE).astype(BF16)
        grad_triple[at : at + WIDE] = dot_nn(key, grad_scores).astype(BF16)
        grad_triple[D + at : D + at + WIDE] = dot_nt(query, grad_scores).astype(BF16)
        grad_triple[2 * D + at : 2 * D + at + WIDE] = dot_nt(grad_out, weights.astype(BF16)).astype(BF16)


def head_back_group(group, x_feat, grad_att, grad_triple, gain, joint, grad_rows, sum_joint, sum_gain):
    values = x_feat[group].astype(F32)
    center = values - mean0(values)
    inv = lax.rsqrt(mean0(center * center) + EPSILON)
    normed = center * inv
    scaled = (normed * gain[...]).astype(BF16)
    sum_joint[...] += dot_nt(grad_triple[...], scaled)
    grad_scaled = dot_nn(joint[...], grad_triple[...])
    sum_gain[...] += grad_scaled * normed
    lifted = grad_scaled * gain[...]
    grad = grad_att[group] + inv * (lifted - mean0(lifted) - normed * mean0(lifted * normed))
    put_group(grad_rows, group, grad)


AXES = ("row", "col")
MESH = pl.DeviceIdType.MESH
POSITIONS = 262144
DEVICES = 128
LANES = 128
BLOCK = 16
STRIDE = 32
SPLIT = STRIDE // GROUPS
ROWS = (D // LANES, GROUPS * TOKENS, LANES)
WHOLE = pl.BlockSpec(memory_space=pltpu.VMEM)


def shape(dims, dtype=BF16):
    return jax.ShapeDtypeStruct(dims, dtype)


def pack(tile, packed):
    def step(a, carry):
        near = tile[a].astype(F32)
        far = tile[STRIDE + a].astype(F32)
        for block in range(SPLIT):
            part = slice(block * GROUPS, block * GROUPS + GROUPS)
            packed[a * SPLIT + block] = jnp.concatenate([near[part], far[part]], axis=0).astype(BF16)
        return carry

    lax.fori_loop(0, STRIDE, step, 0, unroll=2)


def unpack(arrived, tile):
    def step(a, carry):
        blocks = [arrived[a * SPLIT + block].astype(F32) for block in range(SPLIT)]
        tile[a] = jnp.concatenate([b[:GROUPS] for b in blocks], axis=0).astype(BF16)
        tile[STRIDE + a] = jnp.concatenate([b[GROUPS:] for b in blocks], axis=0).astype(BF16)
        return carry

    lax.fori_loop(0, STRIDE, step, 0, unroll=4)


def spread(rows, arrived):
    def step(part, carry):
        values = arrived[pl.ds(part * 8, 8)].astype(F32).reshape(8 * BLOCK, D)
        at = pl.multiple_of(part * 8 * BLOCK, 8 * BLOCK)
        for lane in range(D // LANES):
            rows[lane, pl.ds(at, 8 * BLOCK), :] = values[:, lane * LANES : lane * LANES + LANES]
        return carry

    lax.fori_loop(0, DEVICES // 8, step, 0)


def gather_rows(rows, packed):
    def step(part, carry):
        at = pl.multiple_of(part * 8 * BLOCK, 8 * BLOCK)
        values = jnp.concatenate([rows[lane, pl.ds(at, 8 * BLOCK), :] for lane in range(D // LANES)], axis=1)
        packed[pl.ds(part * 8, 8)] = values.astype(BF16).reshape(8, BLOCK, D)
        return carry

    lax.fori_loop(0, DEVICES // 8, step, 0)


class Place:
    def __init__(self):
        self.row = lax.axis_index("row")
        self.col = lax.axis_index("col")
        self.core = lax.rem(self.col, 2)
        self.other = (self.row, self.col + 1 - 2 * self.core)
        self.slots = (self.col // 2, self.row)
        self.me = self.row * 16 + self.col

    def along(self, half, index):
        return (self.row, index * 2 + self.core) if half == 0 else (index, self.col)

    def apart(self, step):
        jump = lax.rem(step * 45, DEVICES)
        x = lax.rem(lax.rem(self.row, 2) * 2 + self.col // 8 + (jump // 2) % 4, 4)
        y = lax.rem((self.col // 2) % 4 + (jump // 8) % 4, 4)
        z = lax.rem(self.row // 2 + jump // 32, 4)
        core = lax.rem(self.core + jump % 2, 2)
        row = z * 2 + x // 2
        col = (x % 2) * 8 + y * 2 + core
        return row, col


def remote(source, target, sems, index, device):
    return pltpu.make_async_remote_copy(
        src_ref=source, dst_ref=target, send_sem=sems.at[0, index], recv_sem=sems.at[1, index],
        device_id=device, device_id_type=MESH,
    )


def settle(some, sems, side, index):
    pltpu.make_async_copy(some, some, sems.at[side, index]).wait()


def swap_start(place, packed, arrived, sems, index):
    def send(step, carry):
        row, col = place.apart(step)
        remote(packed.at[row * 16 + col], arrived.at[place.me], sems, index, (row, col)).start()
        return carry

    lax.fori_loop(1, DEVICES, send, 0)
    arrived[place.me] = packed[place.me]


def summed(pieces):
    acc = pieces[0].astype(F32)
    for piece in pieces[1:]:
        acc = acc + piece.astype(F32)
    return acc


class DeviceSum:
    def __init__(self, place, sums, total, away, sibling, in_a, part, in_b, sems):
        self.place, self.sums, self.total = place, sums, total
        self.away, self.sibling, self.in_a, self.part, self.in_b, self.sems = away, sibling, in_a, part, in_b, sems
        self.piece = part.shape[1]
        self.half = 8 * self.piece
        self.here = place.core * 2 * self.half

    def rows_of(self, core, half, q):
        start = pl.multiple_of((core * 2 * self.half + half * self.half + q * self.piece) * BLOCK, BLOCK)
        return self.sums[pl.ds(start, self.piece * BLOCK), :]

    def shout(self, source, target, index, half):
        def step(offset, carry):
            q = lax.rem(self.place.slots[half] + offset, 8)
            remote(source(q), target, self.sems, index, self.place.along(half, q)).start()
            return carry

        lax.fori_loop(1, 8, step, 0)

    def start(self):
        for half in range(2):
            def cast(q, carry):
                rows = self.rows_of(1 - self.place.core, half, q).astype(BF16)
                self.away[half, q] = rows.reshape(self.piece, BLOCK, D)
                return carry

            lax.fori_loop(0, 8, cast, 0)
            remote(self.away.at[half], self.sibling.at[half], self.sems, half, self.place.other).start()

    def round_a(self):
        for half in range(2):
            settle(self.away.at[half], self.sems, 0, half)
            settle(self.sibling.at[half], self.sems, 1, half)

            def add(q, carry):
                kept = self.rows_of(self.place.core, half, q).reshape(self.piece, BLOCK, D)
                self.away[half, q] = (kept + self.sibling[half, q].astype(F32)).astype(BF16)
                return carry

            lax.fori_loop(0, 8, add, 0)
            slot = self.place.slots[half]
            self.shout(lambda q: self.away.at[half, q], self.in_a.at[half, slot], 2 + half, half)
            self.in_a[half, slot] = self.away[half, slot]

    def round_b(self):
        for half in range(2):
            settle(self.away.at[half, pl.ds(0, 7)], self.sems, 0, 2 + half)
            settle(self.in_a.at[half, pl.ds(0, 7)], self.sems, 1, 2 + half)

            def add(block, carry):
                self.part[half, block] = summed([self.in_a[half, q, block] for q in range(8)]).astype(BF16)
                return carry

            lax.fori_loop(0, self.piece, add, 0)
            slot = self.place.slots[1 - half]
            self.shout(lambda q: self.part.at[half], self.in_b.at[half, slot], 4 + half, 1 - half)
            self.in_b[half, slot] = self.part[half]

    def round_c(self):
        for half in range(2):
            settle(self.in_b.at[half, pl.ds(0, 7)], self.sems, 0, 4 + half)
            settle(self.in_b.at[half, pl.ds(0, 7)], self.sems, 1, 4 + half)
            base = self.here + half * self.half + self.place.slots[half] * self.piece

            def add(block, carry):
                self.total[base + block] = summed([self.in_b[half, q, block] for q in range(8)]).astype(BF16)
                return carry

            lax.fori_loop(0, self.piece, add, 0)
            spot = self.total.at[pl.ds(base, self.piece)]
            self.shout(lambda q: spot, spot, 6 + half, half)

    def round_d(self):
        for half in range(2):
            seven = self.total.at[pl.ds(0, 7 * self.piece)]
            settle(seven, self.sems, 0, 6 + half)
            settle(seven, self.sems, 1, 6 + half)
            spot = self.total.at[pl.ds(self.here + half * self.half, self.half)]
            remote(spot, spot, self.sems, 8 + half, self.place.other).start()

    def finish(self):
        for half in range(2):
            spot = self.total.at[pl.ds(0, self.half)]
            settle(spot, self.sems, 0, 8 + half)
            settle(spot, self.sems, 1, 8 + half)


def whole_kernel(
    activations, cotangent, first_gain, joint, project, second_gain, expand, reduce,
    block_out, grad_in, total_mlp, total_rest, total_gain,
    packed_a, packed_b, act, cot, rows_a, rows_b,
    gain_a, gain_b, joint_t, project_t, expand_t, reduce_t,
    x_feat, triple, mixed, stats, grad_att, grad_mixed, grad_triple,
    sum_mlp, sum_rest, sum_first, sum_second,
    mlp_away, mlp_sibling, mlp_in_a, mlp_part, mlp_in_b,
    rest_away, rest_sibling, rest_in_a, rest_part, rest_in_b,
    gain_pair, gain_x, gain_y,
    swap_sems, mlp_sems, rest_sems, gain_sems,
):
    place = Place()
    barrier = pltpu.get_barrier_semaphore()

    def greet(step, carry):
        pl.semaphore_signal(barrier, inc=1, device_id=place.apart(step), device_id_type=MESH)
        return carry

    lax.fori_loop(1, DEVICES, greet, 0)
    pack(activations, packed_a)
    pl.semaphore_wait(barrier, DEVICES - 1)
    swap_start(place, packed_a, act, swap_sems, 0)
    pack(cotangent, packed_b)
    swap_start(place, packed_b, cot, swap_sems, 1)
    gain_a[...] = jnp.broadcast_to(first_gain[...], (TOKENS, D)).T
    gain_b[...] = jnp.broadcast_to(second_gain[...], (TOKENS, D)).T
    for natural, turned in ((joint, joint_t), (project, project_t), (expand, expand_t)):
        for start in range(0, natural.shape[1], D):
            turned[start : start + D, :] = natural[:, start : start + D].T
    for start in range(0, FF, D):
        reduce_t[:, start : start + D] = reduce[start : start + D, :].T
    for sums in (sum_mlp, sum_rest, sum_first, sum_second):
        sums[...] = jnp.zeros_like(sums)

    others = pl.ds(0, DEVICES - 1)
    settle(act.at[others], swap_sems, 1, 0)
    spread(rows_a, act)

    def front(group, carry):
        project_group(group, rows_a, gain_a, joint_t, x_feat, triple, stats)
        attend_group(group, triple, mixed, stats)
        return carry

    lax.fori_loop(0, GROUPS, front, 0)
    settle(cot.at[others], swap_sems, 1, 1)
    spread(rows_b, cot)
    sum_project = sum_rest.at[pl.ds(3 * D, D)]
    sum_joint = sum_rest.at[pl.ds(0, 3 * D)]
    sum_expand = sum_mlp.at[pl.ds(0, FF)]
    sum_reduce = sum_mlp.at[pl.ds(FF, FF)]

    def middle(group, carry):
        tail_group(
            group, x_feat, rows_b, mixed, project, project_t, gain_b, expand, expand_t, reduce, reduce_t,
            rows_a, grad_att, grad_mixed, sum_project, sum_expand, sum_reduce, sum_second,
        )
        return carry

    lax.fori_loop(0, GROUPS, middle, 0)
    mlp = DeviceSum(place, sum_mlp, total_mlp, mlp_away, mlp_sibling, mlp_in_a, mlp_part, mlp_in_b, mlp_sems)
    mlp.start()
    settle(packed_a.at[others], swap_sems, 0, 0)
    gather_rows(rows_a, packed_a)
    swap_start(place, packed_a, block_out, swap_sems, 2)

    def back(group, carry):
        for turn, work in ((1, mlp.round_a), (3, mlp.round_b), (5, mlp.round_c), (7, mlp.round_d)):
            pl.when(group == turn)(work)
        attend_back_group(group, triple, stats, grad_mixed, grad_triple)
        head_back_group(group, x_feat, grad_att, grad_triple, gain_a, joint, rows_b, sum_joint, sum_first)
        return carry

    lax.fori_loop(0, GROUPS, back, 0)
    rest = DeviceSum(place, sum_rest, total_rest, rest_away, rest_sibling, rest_in_a, rest_part, rest_in_b, rest_sems)
    rest.start()
    both = [jnp.sum(sums[...].T, axis=0, keepdims=True) for sums in (sum_first, sum_second)]
    gain_pair[0] = jnp.concatenate(both + [jnp.zeros((6, D), F32)], axis=0)
    gain_first = remote(gain_pair.at[0], gain_pair.at[1], gain_sems, 0, place.other)
    gain_first.start()
    settle(packed_b.at[others], swap_sems, 0, 1)
    gather_rows(rows_b, packed_b)
    swap_start(place, packed_b, grad_in, swap_sems, 3)
    mlp.finish()

    def gain_round(values, slots, index, half):
        slot = place.slots[half]
        slots[slot] = values

        def step(offset, carry):
            q = lax.rem(slot + offset, 8)
            remote(slots.at[slot], slots.at[slot], gain_sems, index, place.along(half, q)).start()
            return carry

        lax.fori_loop(1, 8, step, 0)

    def gain_sum(slots, index):
        settle(slots.at[pl.ds(0, 7)], gain_sems, 0, index)
        settle(slots.at[pl.ds(0, 7)], gain_sems, 1, index)
        return summed([slots[q] for q in range(8)])

    rest.round_a()
    gain_first.wait()
    gain_round(gain_pair[0] + gain_pair[1], gain_x, 1, 0)
    rest.round_b()
    gain_round(gain_sum(gain_x, 1), gain_y, 2, 1)
    rest.round_c()
    total_gain[...] = gain_sum(gain_y, 2)
    rest.round_d()
    settle(packed_a.at[others], swap_sems, 0, 2)
    settle(block_out.at[others], swap_sems, 1, 2)
    settle(packed_b.at[others], swap_sems, 0, 3)
    settle(grad_in.at[others], swap_sems, 1, 3)
    rest.finish()


def finish_kernel(out_blocks, grad_blocks, mlp, rest, gains, block_out, grad_in, g_joint, g_project, g_expand, g_reduce, g_first, g_second):
    factor = float(POSITIONS) ** -0.5
    unpack(out_blocks, block_out)
    unpack(grad_blocks, grad_in)

    def natural(source, at, count):
        return source[at : at + count].astype(F32).reshape(count * BLOCK, D) * factor

    step = D // BLOCK
    for part in range(FF // D):
        span = slice(part * D, part * D + D)
        g_expand[:, span] = natural(mlp, part * step, step).T
        g_reduce[span, :] = natural(mlp, FF // BLOCK + part * step, step)
    for part in range(3):
        g_joint[:, part * D : part * D + D] = natural(rest, part * step, step).T
    g_project[...] = natural(rest, 3 * step, step)
    g_first[...] = gains[0:1] * factor
    g_second[...] = gains[1:2] * factor


def shards(
    activations, cotangent, first_gain, joint_weight, output_weight, second_gain, expand_weight, reduce_weight
):
    dma = pltpu.SemaphoreType.DMA
    blocks = (DEVICES, BLOCK, D)
    feat = (GROUPS, D, TOKENS)
    mlp, rest = 2 * FF, 4 * D

    def sum_scratch(rows):
        piece = rows // 32 // BLOCK
        spread_out = (2, 8, piece, BLOCK, D)
        return [
            pltpu.VMEM(spread_out, BF16), pltpu.VMEM(spread_out, BF16), pltpu.VMEM(spread_out, BF16),
            pltpu.VMEM((2, piece, BLOCK, D), BF16), pltpu.VMEM(spread_out, BF16),
        ]

    out_blocks, grad_blocks, total_mlp, total_rest, total_gain = pl.pallas_call(
        whole_kernel,
        in_specs=[WHOLE] * 8,
        out_specs=[WHOLE] * 5,
        out_shape=[
            shape(blocks), shape(blocks), shape((mlp // BLOCK, BLOCK, D)), shape((rest // BLOCK, BLOCK, D)),
            shape((8, D), F32),
        ],
        scratch_shapes=[
            pltpu.VMEM(blocks, BF16), pltpu.VMEM(blocks, BF16), pltpu.VMEM(blocks, BF16), pltpu.VMEM(blocks, BF16),
            pltpu.VMEM(ROWS, F32), pltpu.VMEM(ROWS, F32),
            pltpu.VMEM((D, TOKENS), F32), pltpu.VMEM((D, TOKENS), F32),
            pltpu.VMEM((3 * D, D), BF16), pltpu.VMEM((D, D), BF16), pltpu.VMEM((FF, D), BF16), pltpu.VMEM((D, FF), BF16),
            pltpu.VMEM(feat, BF16), pltpu.VMEM((GROUPS, 3 * D, TOKENS), BF16), pltpu.VMEM(feat, BF16),
            pltpu.VMEM((GROUPS, 2 * HEADS, TOKENS), F32), pltpu.VMEM(feat, F32), pltpu.VMEM(feat, BF16),
            pltpu.VMEM((3 * D, TOKENS), BF16),
            pltpu.VMEM((mlp, D), F32), pltpu.VMEM((rest, D), F32), pltpu.VMEM((D, TOKENS), F32), pltpu.VMEM((D, TOKENS), F32),
            *sum_scratch(mlp), *sum_scratch(rest),
            pltpu.VMEM((2, 8, D), F32), pltpu.VMEM((8, 8, D), F32), pltpu.VMEM((8, 8, D), F32),
            dma((2, 4)), dma((2, 10)), dma((2, 10)), dma((2, 3)),
        ],
        cost_estimate=pl.CostEstimate(flops=12 * 10**10, bytes_accessed=10**8, transcendentals=0),
        compiler_params=pltpu.CompilerParams(
            collective_id=0, has_side_effects=True, vmem_limit_bytes=63 * 2**20
        ),
    )(
        activations, cotangent, first_gain[None, :], joint_weight, output_weight, second_gain[None, :],
        expand_weight, reduce_weight,
    )
    tile = activations.shape
    outs = [
        shape(tile), shape(tile), shape((D, 3 * D), F32), shape((D, D), F32), shape((D, FF), F32), shape((FF, D), F32),
        shape((1, D), F32), shape((1, D), F32),
    ]
    results = pl.pallas_call(
        finish_kernel,
        in_specs=[WHOLE] * 5,
        out_specs=[WHOLE] * len(outs),
        out_shape=outs,
        compiler_params=pltpu.CompilerParams(vmem_limit_bytes=48 * 2**20),
    )(out_blocks, grad_blocks, total_mlp, total_rest, total_gain)
    return tuple(results[:6]) + (results[6][0], results[7][0])


def solution(mesh):
    tile = P("row", "col", None)
    return jax.shard_map(
        shards,
        mesh=mesh,
        in_specs=(tile, tile) + (P(),) * 6,
        out_specs=(tile, tile) + (P(),) * 6,
        check_vma=False,
    )
```

time: 318 us -> 238 us (0.75)
  blocking collectives: 34.6 us -> 0 us
  starting transfers between devices: 22.1 us -> 0 us
  waiting for transfers between devices: 14.1 us -> 0 us
  Pallas kernels: 222 us -> 229 us
  local copies, waits for them, and re-layouts: 13.9 us -> 7.27 us
  other arithmetic: 7.12 us -> 1.19 us
    all_to_all x1 -> x0, blocking collectives: 34.6 us -> none  [swap(): return lax.all_to_all(blocks, AXES, split_axis=0, concat_axis=0, tiled=True)]
    all_to_all x3 -> x0, starting transfers between devices: 22.1 us -> none  [swap(): return lax.all_to_all(blocks, AXES, split_axis=0, concat_axis=0, tiled=True)]
    all_to_all x3 -> x0, waiting for transfers between devices: 14.1 us -> none  [swap(): return lax.all_to_all(blocks, AXES, split_axis=0, concat_axis=0, tiled=True)]
    mul x4 -> x0, other arithmetic: 7.04 us -> none  [the longest x3 6.44 us: cut(): sides[:, start:start + size].reshape(2 * size, D).astype(F32) * factor]
    pallas_call x8 -> x2, Pallas kernels: 222 us -> 229 us  [the longest x1 223 us: shards(): pl.pallas_call(whole_kernel, in_specs=[WHOLE] * 8, out_specs=[WHOLE] * 5,...]
    unnamed x31 -> x8, local copies, waits for them, and re-layouts: 10.3 us -> 4.78 us
  transfers between devices with their start and end apart: 3 -> 0, of which waited for: 1 -> 0; matrix products, arithmetic and copies ran while one was open for 6% -> 0% of each run, Pallas kernels for 41% -> 0%
where the time goes in v3:
time: 238 us
  Pallas kernels  229 us (96%)
  local copies, waits for them, and re-layouts  7.27 us (3%)
    pallas_call x1, Pallas kernels, shards(): pl.pallas_call(whole_kernel, in_specs=[WHOLE] * 8, out_specs=[WHOLE] * 5,...  223 us
    pallas_call x1, Pallas kernels, shards(): pl.pallas_call(finish_kernel, in_specs=[WHOLE] * 5, out_specs=[WHOLE] * l...  6.05 us
    unnamed x8, local copies, waits for them, and re-layouts  4.78 us

profile of v3, /device:TPU:1, one launch (start us, length us, event | category | flops | bytes accessed | tf_op | source)
XLA Modules:
  0.0 237.8 jit_solution(8636047532460429497)
XLA Ops:
  0.6 1.2 broadcast_in_dim.6.first_gain
  1.9 1.2 broadcast_in_dim.7.second_gain
  3.1 222.6 %shard_map.143 = (bf16[128,16,384]{2,1,0:T(8,128)(2,1)}, bf16[128,16,384]{2,1,0:T(8,128)(2,1)}, bf16[192,16,384]{2,1,0:T(8,128)(2,1)}, bf16[96,16,384]{2,1,0:T(8,128)(2,1)}, f32[8,384]{1,0:T(8,128)}) custom-call(bf16[64,32,384]{2,1,0:T(8,128)(2,1)} %activations.1, bf16[64,32,384]{2,1,0:T(8,128)(2,1)} %cotangent.1, f32[1,384]{1,0:T(1,128)} %broadcast_in_dim.6.first_gain, ...), custom_call_target="tpu_custom_call" | custom-call | flops 120000004096 | bytes 100000000 | tf_op jit(solution)/shard_map/pallas_call | solution.py:506
  225.8 0.0 copy-start
  225.8 1.4 copy-done
  227.2 0.0 copy-start.1
  227.2 1.4 copy-done.1
  228.6 0.0 copy-start.2
  228.6 1.3 copy-done.2
  229.9 0.0 copy-start.3
  229.9 0.7 copy-done.3
  230.6 6.1 %shard_map.144 = (bf16[64,32,384]{2,1,0:T(8,128)(2,1)}, bf16[64,32,384]{2,1,0:T(8,128)(2,1)}, f32[384,1152]{1,0:T(8,128)}, f32[384,384]{1,0:T(8,128)}, f32[384,1...) custom-call(bf16[128,16,384]{2,1,0:T(8,128)(2,1)S(1)} %copy-done, ...), custom_call_target="tpu_custom_call" | custom-call | tf_op jit(solution)/shard_map/pallas_call | solution.py:540
  236.6 0.6 reduce.1
  237.2 0.6 reduce.2
Async XLA Ops:
  225.8 1.4 copy-start
  227.2 1.4 copy-start.1
  228.6 1.3 copy-start.2
  229.9 0.7 copy-start.3

commit v4 on v3

v4 whole, which is shorter than its diff:
```python
import jax
import jax.numpy as jnp
from jax import lax
from jax.experimental import pallas as pl
from jax.experimental.pallas import tpu as pltpu
from jax.sharding import PartitionSpec as P

HEADS = 12
GRID = 16
GROUPS = 8
TOKENS = 256
D = 384
FF = 1536
WIDE = 32
CHUNK = 512

EPSILON = 1e-05
SQRT_HALF = 0.7071067811865476
INV_ROOT_TAU = 0.3989422804014327
LOG2E = 1.4426950408889634
SCORE_SCALE = WIDE ** (-0.5)
F32 = jnp.float32
BF16 = jnp.bfloat16


def dot_nn(a, b):
    return lax.dot_general(a, b, (((1,), (0,)), ((), ())), preferred_element_type=F32)


def dot_nt(a, b):
    return lax.dot_general(a, b, (((1,), (1,)), ((), ())), preferred_element_type=F32)


def dot_tn(a, b):
    return lax.dot_general(a, b, (((0,), (0,)), ((), ())), preferred_element_type=F32)


def mean0(values):
    return jnp.sum(values, axis=0, keepdims=True) * (1.0 / D)


def gelu_parts(pre):
    gauss = jnp.exp2(pre * pre * (-0.5 * LOG2E))
    t = 1.0 / (1.0 + (0.3275911 * SQRT_HALF) * jnp.abs(pre))
    poly = t * (0.127414796 + t * (-0.142248368 + t * (0.7107068705 + t * (-0.7265760135 + t * 0.5307027145))))
    tail = poly * gauss
    cdf = jnp.where(pre >= 0.0, 1.0 - tail, tail)
    return pre * cdf, cdf + pre * gauss * INV_ROOT_TAU


def members(group):
    start = (group // (GROUPS // 2)) * (GROUPS // 2 * TOKENS) + lax.rem(group, GROUPS // 2)
    return pl.ds(start, TOKENS, stride=GROUPS // 2)


def take_group(rows, group):
    return jnp.concatenate([rows[lane, members(group), :].T for lane in range(D // 128)], axis=0)


def put_group(rows, group, values):
    for lane in range(D // 128):
        rows[lane, members(group), :] = values[lane * 128 : lane * 128 + 128].T


def project_group(group, x_rows, gain, joint_t, x_feat, scaled_first, triple):
    values = take_group(x_rows, group)
    x_feat[group] = values.astype(BF16)
    center = values - mean0(values)
    inv = lax.rsqrt(mean0(center * center) + EPSILON)
    scaled = (center * inv * gain[...]).astype(BF16)
    scaled_first[group] = scaled
    triple[group] = dot_nn(joint_t[...], scaled).astype(BF16)


def head_scores(triple, group, head):
    at = head * WIDE
    query = triple[group, at : at + WIDE]
    key = triple[group, D + at : D + at + WIDE]
    return dot_tn(key, query) * (SCORE_SCALE * LOG2E)


def attend_group(group, triple, mixed, stats):
    ahead = head_scores(triple, group, 0)
    for head in range(HEADS):
        at = head * WIDE
        scores = ahead
        if head + 1 < HEADS:
            ahead = head_scores(triple, group, head + 1)
        value = triple[group, 2 * D + at : 2 * D + at + WIDE]
        top = jnp.max(scores, axis=0, keepdims=True)
        raised = jnp.exp2(scores - top)
        share = 1.0 / jnp.sum(raised, axis=0, keepdims=True)
        stats[group, 2 * head : 2 * head + 1] = top
        stats[group, 2 * head + 1 : 2 * head + 2] = share
        weights = (raised * share).astype(BF16)
        mixed[group, at : at + WIDE] = dot_nn(value, weights).astype(BF16)


def tail_group(
    group, x_feat, cot_rows, mixed, project, project_t, gain, expand, expand_t, reduce, reduce_t,
    result_rows, grad_att, grad_mixed, sum_project, sum_expand, sum_reduce, sum_gain,
):
    blend = mixed[group]
    cot32 = take_group(cot_rows, group)
    cot = cot32.astype(BF16)
    attended = x_feat[group].astype(F32) + dot_nn(project_t[...], blend)
    center = attended - mean0(attended)
    inv = lax.rsqrt(mean0(center * center) + EPSILON)
    normed = center * inv
    scaled = (normed * gain[...]).astype(BF16)
    result = attended
    grad_scaled = None
    def chunk_pair(start):
        part = slice(start, start + CHUNK)
        return dot_nn(expand_t[part, :], scaled), dot_nn(reduce[part, :], cot)

    ahead = chunk_pair(0)
    for start in range(0, FF, CHUNK):
        part = slice(start, start + CHUNK)
        pre, grad_hidden = ahead
        if start + CHUNK < FF:
            ahead = chunk_pair(start + CHUNK)
        value, slope = gelu_parts(pre)
        hidden = value.astype(BF16)
        grad_pre = (grad_hidden.astype(BF16).astype(F32) * slope).astype(BF16)
        result = result + dot_nn(reduce_t[:, part], hidden)
        back = dot_nn(expand[:, part], grad_pre)
        grad_scaled = back if grad_scaled is None else grad_scaled + back
        sum_reduce[part, :] += dot_nt(hidden, cot)
        sum_expand[part, :] += dot_nt(grad_pre, scaled)
    put_group(result_rows, group, result)
    sum_gain[...] += grad_scaled * normed
    lifted = grad_scaled * gain[...]
    grad = cot32 + inv * (lifted - mean0(lifted) - normed * mean0(lifted * normed))
    grad_att[group] = grad
    grad_b = grad.astype(BF16)
    sum_project[...] += dot_nt(blend, grad_b)
    grad_mixed[group] = dot_nn(project[...], grad_b).astype(BF16)


def head_pair(triple, grad_mixed, group, head):
    at = head * WIDE
    value = triple[group, 2 * D + at : 2 * D + at + WIDE]
    return head_scores(triple, group, head), dot_tn(value, grad_mixed[group, at : at + WIDE])


def attend_back_group(group, scaled_first, triple, stats, grad_mixed, grad_triple, sum_joint):
    def spill(head, grad_scores, weights):
        at = head * WIDE
        query = triple[group, at : at + WIDE]
        key = triple[group, D + at : D + at + WIDE]
        grad_out = grad_mixed[group, at : at + WIDE]
        grad_triple[at : at + WIDE] = dot_nn(key, grad_scores).astype(BF16)
        grad_triple[D + at : D + at + WIDE] = dot_nt(query, grad_scores).astype(BF16)
        grad_triple[2 * D + at : 2 * D + at + WIDE] = dot_nt(grad_out, weights).astype(BF16)

    ahead = head_pair(triple, grad_mixed, group, 0)
    for head in range(HEADS):
        scores, grad_weights = ahead
        if head + 1 < HEADS:
            ahead = head_pair(triple, grad_mixed, group, head + 1)
        top = stats[group, 2 * head : 2 * head + 1]
        share = stats[group, 2 * head + 1 : 2 * head + 2]
        weights = jnp.exp2(scores - top) * share
        inner = jnp.sum(weights * grad_weights, axis=0, keepdims=True)
        grad_scores = (weights * (grad_weights - inner) * SCORE_SCALE).astype(BF16)
        spill(head, grad_scores, weights.astype(BF16))
    triple[group] = grad_triple[...]
    sum_joint[...] += dot_nt(grad_triple[...], scaled_first[group])


def head_back_group(group, x_feat, grad_att, grad_triple, gain, joint, grad_rows, sum_gain):
    values = x_feat[group].astype(F32)
    center = values - mean0(values)
    inv = lax.rsqrt(mean0(center * center) + EPSILON)
    normed = center * inv
    grad_scaled = dot_nn(joint[...], grad_triple[group])
    sum_gain[...] += grad_scaled * normed
    lifted = grad_scaled * gain[...]
    grad = grad_att[group] + inv * (lifted - mean0(lifted) - normed * mean0(lifted * normed))
    put_group(grad_rows, group, grad)


AXES = ("row", "col")
MESH = pl.DeviceIdType.MESH
POSITIONS = 262144
DEVICES = 128
LANES = 128
BLOCK = 8
TALL = 16
STRIDE = 32
SPLIT = STRIDE // GROUPS
ROWS = (D // LANES, GROUPS * TOKENS, LANES)
WHOLE = pl.BlockSpec(memory_space=pltpu.VMEM)


def shape(dims, dtype=BF16):
    return jax.ShapeDtypeStruct(dims, dtype)


def pack(tile, packed):
    few = GROUPS // 2

    def step(a, carry):
        near = tile[a].astype(F32)
        far = tile[STRIDE + a].astype(F32)
        for block in range(SPLIT):
            for half in range(2):
                at = block * GROUPS + half * few
                both = jnp.concatenate([near[at : at + few], far[at : at + few]], axis=0)
                packed[half, a * SPLIT + block] = both.astype(BF16)
        return carry

    lax.fori_loop(0, STRIDE, step, 0, unroll=2)


def spread(rows, arrived, half):
    def step(part, carry):
        values = arrived[half, pl.ds(part * 16, 16)].astype(F32).reshape(16 * BLOCK, D)
        at = pl.multiple_of((half * DEVICES + part * 16) * BLOCK, 16 * BLOCK)
        for lane in range(D // LANES):
            rows[lane, pl.ds(at, 16 * BLOCK), :] = values[:, lane * LANES : lane * LANES + LANES]
        return carry

    lax.fori_loop(0, DEVICES // 16, step, 0)


def gather_rows(rows, packed, half):
    def step(part, carry):
        at = pl.multiple_of((half * DEVICES + part * 16) * BLOCK, 16 * BLOCK)
        values = jnp.concatenate([rows[lane, pl.ds(at, 16 * BLOCK), :] for lane in range(D // LANES)], axis=1)
        packed[half, pl.ds(part * 16, 16)] = values.reshape(16, BLOCK, D).astype(BF16)
        return carry

    lax.fori_loop(0, DEVICES // 16, step, 0)


class Place:
    def __init__(self):
        self.row = lax.axis_index("row")
        self.col = lax.axis_index("col")
        self.core = lax.rem(self.col, 2)
        self.other = (self.row, self.col + 1 - 2 * self.core)
        self.slots = (self.col // 2, self.row)
        self.me = self.row * 16 + self.col

    def along(self, half, index):
        return (self.row, index * 2 + self.core) if half == 0 else (index, self.col)

    def apart(self, step):
        jump = lax.rem(step * 45, DEVICES)
        x = lax.rem(lax.rem(self.row, 2) * 2 + self.col // 8 + (jump // 2) % 4, 4)
        y = lax.rem((self.col // 2) % 4 + (jump // 8) % 4, 4)
        z = lax.rem(self.row // 2 + jump // 32, 4)
        core = lax.rem(self.core + jump % 2, 2)
        row = z * 2 + x // 2
        col = (x % 2) * 8 + y * 2 + core
        return row, col


def remote(source, target, sems, index, device):
    return pltpu.make_async_remote_copy(
        src_ref=source, dst_ref=target, send_sem=sems.at[0, index], recv_sem=sems.at[1, index],
        device_id=device, device_id_type=MESH,
    )


def settle(some, sems, side, index):
    pltpu.make_async_copy(some, some, sems.at[side, index]).wait()


def swap_start(place, packed, arrived, sems, which, half):
    def send(step, carry):
        row, col = place.apart(step)
        source, target = packed.at[half, row * 16 + col], arrived.at[half, place.me]
        remote(source, target, sems, which * 2 + half, (row, col)).start()
        return carry

    lax.fori_loop(1, DEVICES, send, 0)
    arrived[half, place.me] = packed[half, place.me]


def swap_wait(some, sems, side, which, half):
    settle(some.at[half, pl.ds(0, DEVICES - 1)], sems, side, which * 2 + half)


def summed(pieces):
    acc = pieces[0].astype(F32)
    for piece in pieces[1:]:
        acc = acc + piece.astype(F32)
    return acc


class DeviceSum:
    def __init__(self, place, sums, total, away, sibling, in_a, part, in_b, sems):
        self.place, self.sums, self.total = place, sums, total
        self.away, self.sibling, self.in_a, self.part, self.in_b, self.sems = away, sibling, in_a, part, in_b, sems
        self.piece = part.shape[1]
        self.half = 8 * self.piece
        self.here = place.core * 2 * self.half

    def rows_of(self, core, half, q):
        start = pl.multiple_of((core * 2 * self.half + half * self.half + q * self.piece) * TALL, TALL)
        return self.sums[pl.ds(start, self.piece * TALL), :]

    def shout(self, source, target, index, half):
        def step(offset, carry):
            q = lax.rem(self.place.slots[half] + offset, 8)
            remote(source(q), target, self.sems, index, self.place.along(half, q)).start()
            return carry

        lax.fori_loop(1, 8, step, 0)

    def start(self):
        for half in range(2):
            def cast(q, carry):
                rows = self.rows_of(1 - self.place.core, half, q).astype(BF16)
                self.away[half, q] = rows.reshape(self.piece, TALL, D)
                return carry

            lax.fori_loop(0, 8, cast, 0)
            remote(self.away.at[half], self.sibling.at[half], self.sems, half, self.place.other).start()

    def round_a(self):
        for half in range(2):
            settle(self.away.at[half], self.sems, 0, half)
            settle(self.sibling.at[half], self.sems, 1, half)

            def add(q, carry):
                kept = self.rows_of(self.place.core, half, q).reshape(self.piece, TALL, D)
                self.away[half, q] = (kept + self.sibling[half, q].astype(F32)).astype(BF16)
                return carry

            lax.fori_loop(0, 8, add, 0)
            slot = self.place.slots[half]
            self.shout(lambda q: self.away.at[half, q], self.in_a.at[half, slot], 2 + half, half)
            self.in_a[half, slot] = self.away[half, slot]

    def round_b(self):
        for half in range(2):
            settle(self.away.at[half, pl.ds(0, 7)], self.sems, 0, 2 + half)
            settle(self.in_a.at[half, pl.ds(0, 7)], self.sems, 1, 2 + half)

            def add(block, carry):
                self.part[half, block] = summed([self.in_a[half, q, block] for q in range(8)]).astype(BF16)
                return carry

            lax.fori_loop(0, self.piece, add, 0)
            slot = self.place.slots[1 - half]
            self.shout(lambda q: self.part.at[half], self.in_b.at[half, slot], 4 + half, 1 - half)
            self.in_b[half, slot] = self.part[half]

    def round_c(self):
        for half in range(2):
            settle(self.in_b.at[half, pl.ds(0, 7)], self.sems, 0, 4 + half)
            settle(self.in_b.at[half, pl.ds(0, 7)], self.sems, 1, 4 + half)
            base = self.here + half * self.half + self.place.slots[half] * self.piece

            def add(block, carry):
                self.total[base + block] = summed([self.in_b[half, q, block] for q in range(8)]).astype(BF16)
                return carry

            lax.fori_loop(0, self.piece, add, 0)
            spot = self.total.at[pl.ds(base, self.piece)]
            self.shout(lambda q: spot, spot, 6 + half, half)

    def round_d(self):
        for half in range(2):
            seven = self.total.at[pl.ds(0, 7 * self.piece)]
            settle(seven, self.sems, 0, 6 + half)
            settle(seven, self.sems, 1, 6 + half)
            spot = self.total.at[pl.ds(self.here + half * self.half, self.half)]
            remote(spot, spot, self.sems, 8 + half, self.place.other).start()

    def finish(self):
        for half in range(2):
            spot = self.total.at[pl.ds(0, self.half)]
            settle(spot, self.sems, 0, 8 + half)
            settle(spot, self.sems, 1, 8 + half)


def whole_kernel(
    activations, cotangent, first_gain, joint, project, second_gain, expand, reduce,
    block_out, grad_in, total_mlp, total_rest, total_gain,
    packed_a, packed_b, act, cot, rows_a, rows_b,
    gain_a, gain_b, joint_t, project_t, expand_t, reduce_t,
    x_feat, scaled_first, triple, mixed, stats, grad_att, grad_mixed, grad_triple,
    sum_mlp, sum_rest, sum_first, sum_second,
    mlp_away, mlp_sibling, mlp_in_a, mlp_part, mlp_in_b,
    rest_away, rest_sibling, rest_in_a, rest_part, rest_in_b,
    gain_pair, gain_x, gain_y,
    swap_sems, mlp_sems, rest_sems, gain_sems,
):
    place = Place()
    barrier = pltpu.get_barrier_semaphore()

    def greet(step, carry):
        pl.semaphore_signal(barrier, inc=1, device_id=place.apart(step), device_id_type=MESH)
        return carry

    lax.fori_loop(1, DEVICES, greet, 0)
    pack(activations, packed_a)
    pl.semaphore_wait(barrier, DEVICES - 1)
    for half in range(2):
        swap_start(place, packed_a, act, swap_sems, 0, half)
    pack(cotangent, packed_b)
    for half in range(2):
        swap_start(place, packed_b, cot, swap_sems, 1, half)
    gain_a[...] = jnp.broadcast_to(first_gain[...].reshape(1, D), (TOKENS, D)).T
    gain_b[...] = jnp.broadcast_to(second_gain[...].reshape(1, D), (TOKENS, D)).T
    for natural, turned in ((joint, joint_t), (project, project_t), (expand, expand_t)):
        for start in range(0, natural.shape[1], D):
            turned[start : start + D, :] = natural[:, start : start + D].T
    for start in range(0, FF, D):
        reduce_t[:, start : start + D] = reduce[start : start + D, :].T
    for sums in (sum_mlp, sum_rest, sum_first, sum_second):
        sums[...] = jnp.zeros_like(sums)

    def by_halves(work):
        def step(half, carry):
            work(half)
            return carry

        lax.fori_loop(0, 2, step, 0)

    def groups_of(half, work):
        def step(group, carry):
            work(group)
            return carry

        lax.fori_loop(half * (GROUPS // 2), half * (GROUPS // 2) + GROUPS // 2, step, 0)

    def front(half):
        swap_wait(act, swap_sems, 1, 0, half)
        spread(rows_a, act, half)

        def work(group):
            project_group(group, rows_a, gain_a, joint_t, x_feat, scaled_first, triple)
            attend_group(group, triple, mixed, stats)

        groups_of(half, work)

    by_halves(front)
    for half in range(2):
        swap_wait(packed_a, swap_sems, 0, 0, half)
    sum_project = sum_rest.at[pl.ds(3 * D, D)]
    sum_joint = sum_rest.at[pl.ds(0, 3 * D)]
    sum_expand = sum_mlp.at[pl.ds(0, FF)]
    sum_reduce = sum_mlp.at[pl.ds(FF, FF)]

    def middle(half):
        swap_wait(cot, swap_sems, 1, 1, half)
        spread(rows_b, cot, half)

        def work(group):
            tail_group(
                group, x_feat, rows_b, mixed, project, project_t, gain_b, expand, expand_t, reduce, reduce_t,
                rows_a, grad_att, grad_mixed, sum_project, sum_expand, sum_reduce, sum_second,
            )

        groups_of(half, work)
        gather_rows(rows_a, packed_a, half)
        swap_start(place, packed_a, block_out, swap_sems, 2, half)

    by_halves(middle)
    for half in range(2):
        swap_wait(packed_b, swap_sems, 0, 1, half)
    mlp = DeviceSum(place, sum_mlp, total_mlp, mlp_away, mlp_sibling, mlp_in_a, mlp_part, mlp_in_b, mlp_sems)
    rest = DeviceSum(place, sum_rest, total_rest, rest_away, rest_sibling, rest_in_a, rest_part, rest_in_b, rest_sems)
    mlp.start()

    def back(half):
        def attention(group):
            for turn, work in ((1, mlp.round_a), (3, mlp.round_b), (5, mlp.round_c), (7, mlp.round_d)):
                pl.when(group == turn)(work)
            attend_back_group(group, scaled_first, triple, stats, grad_mixed, grad_triple, sum_joint)

        groups_of(half, attention)
        pl.when(half == 1)(rest.start)

        def head(group):
            pl.when(group == 7)(rest.round_a)
            head_back_group(group, x_feat, grad_att, triple, gain_a, joint, rows_b, sum_first)

        groups_of(half, head)
        gather_rows(rows_b, packed_b, half)
        swap_start(place, packed_b, grad_in, swap_sems, 3, half)

    by_halves(back)
    both = [jnp.sum(sums[...].T, axis=0, keepdims=True) for sums in (sum_first, sum_second)]
    gain_pair[0] = jnp.concatenate(both + [jnp.zeros((6, D), F32)], axis=0)
    gain_first = remote(gain_pair.at[0], gain_pair.at[1], gain_sems, 0, place.other)
    gain_first.start()

    def gain_round(values, slots, index, half):
        slot = place.slots[half]
        slots[slot] = values

        def step(offset, carry):
            q = lax.rem(slot + offset, 8)
            remote(slots.at[slot], slots.at[slot], gain_sems, index, place.along(half, q)).start()
            return carry

        lax.fori_loop(1, 8, step, 0)

    def gain_sum(slots, index):
        settle(slots.at[pl.ds(0, 7)], gain_sems, 0, index)
        settle(slots.at[pl.ds(0, 7)], gain_sems, 1, index)
        return summed([slots[q] for q in range(8)])

    rest.round_b()
    gain_first.wait()
    gain_round(gain_pair[0] + gain_pair[1], gain_x, 1, 0)
    rest.round_c()
    gain_round(gain_sum(gain_x, 1), gain_y, 2, 1)
    rest.round_d()
    total_gain[...] = gain_sum(gain_y, 2)
    mlp.finish()
    for packed, arrived, which in ((packed_a, block_out, 2), (packed_b, grad_in, 3)):
        for half in range(2):
            swap_wait(packed, swap_sems, 0, which, half)
            swap_wait(arrived, swap_sems, 1, which, half)
    rest.finish()


PARTS = 4


def finish_kernel(
    out_blocks, grad_blocks, expand, reduce, joint, project, gains,
    block_out, grad_in, g_joint, g_project, g_expand, g_reduce, g_first, g_second,
):
    factor = float(POSITIONS) ** -0.5
    few = GROUPS // 2
    for arrived, tile in ((out_blocks, block_out), (grad_blocks, grad_in)):
        for a in range(STRIDE // PARTS):
            early = [arrived[0, a * SPLIT + block].astype(F32) for block in range(SPLIT)]
            late = [arrived[1, a * SPLIT + block].astype(F32) for block in range(SPLIT)]
            for side in range(2):
                part = slice(side * few, side * few + few)
                pieces = [piece[part] for pair in zip(early, late) for piece in pair]
                tile[side, a] = jnp.concatenate(pieces, axis=0).astype(BF16)

    def natural(source):
        return source[...].astype(F32).reshape(D, D) * factor

    g_expand[...] = natural(expand).T
    g_reduce[...] = natural(reduce)
    g_joint[...] = natural(joint).T
    g_project[...] = natural(project)
    g_first[...] = gains[0] * factor
    g_second[...] = gains[1] * factor


def shards(
    activations, cotangent, first_gain, joint_weight, output_weight, second_gain, expand_weight, reduce_weight
):
    dma = pltpu.SemaphoreType.DMA
    blocks = (2, DEVICES, BLOCK, D)
    feat = (GROUPS, D, TOKENS)
    mlp, rest = 2 * FF, 4 * D

    def sum_scratch(rows):
        piece = rows // 32 // TALL
        spread_out = (2, 8, piece, TALL, D)
        return [
            pltpu.VMEM(spread_out, BF16), pltpu.VMEM(spread_out, BF16), pltpu.VMEM(spread_out, BF16),
            pltpu.VMEM((2, piece, TALL, D), BF16), pltpu.VMEM(spread_out, BF16),
        ]

    out_blocks, grad_blocks, total_mlp, total_rest, total_gain = pl.pallas_call(
        whole_kernel,
        in_specs=[WHOLE] * 8,
        out_specs=[WHOLE] * 5,
        out_shape=[
            shape(blocks), shape(blocks), shape((mlp // TALL, TALL, D)), shape((rest // TALL, TALL, D)),
            shape((8, D), F32),
        ],
        scratch_shapes=[
            pltpu.VMEM(blocks, BF16), pltpu.VMEM(blocks, BF16), pltpu.VMEM(blocks, BF16), pltpu.VMEM(blocks, BF16),
            pltpu.VMEM(ROWS, F32), pltpu.VMEM(ROWS, F32),
            pltpu.VMEM((D, TOKENS), F32), pltpu.VMEM((D, TOKENS), F32),
            pltpu.VMEM((3 * D, D), BF16), pltpu.VMEM((D, D), BF16), pltpu.VMEM((FF, D), BF16), pltpu.VMEM((D, FF), BF16),
            pltpu.VMEM(feat, BF16), pltpu.VMEM(feat, BF16), pltpu.VMEM((GROUPS, 3 * D, TOKENS), BF16),
            pltpu.VMEM(feat, BF16), pltpu.VMEM((GROUPS, 2 * HEADS, TOKENS), F32), pltpu.VMEM(feat, F32),
            pltpu.VMEM(feat, BF16), pltpu.VMEM((3 * D, TOKENS), BF16),
            pltpu.VMEM((mlp, D), F32), pltpu.VMEM((rest, D), F32), pltpu.VMEM((D, TOKENS), F32), pltpu.VMEM((D, TOKENS), F32),
            *sum_scratch(mlp), *sum_scratch(rest),
            pltpu.VMEM((2, 8, D), F32), pltpu.VMEM((8, 8, D), F32), pltpu.VMEM((8, 8, D), F32),
            dma((2, 8)), dma((2, 10)), dma((2, 10)), dma((2, 3)),
        ],
        cost_estimate=pl.CostEstimate(flops=12 * 10**10, bytes_accessed=10**8, transcendentals=0),
        compiler_params=pltpu.CompilerParams(
            collective_id=0, has_side_effects=True, vmem_limit_bytes=63 * 2**20
        ),
    )(
        activations, cotangent, first_gain, joint_weight, output_weight, second_gain, expand_weight, reduce_weight,
    )
    tile = (2, STRIDE, STRIDE, D)
    last = 3 * D // D - 1
    arrived = pl.BlockSpec((2, DEVICES // PARTS, BLOCK, D), lambda i: (0, i, 0, 0))
    placed = pl.BlockSpec((2, STRIDE // PARTS, STRIDE, D), lambda i: (0, i, 0, 0))

    def sums(index):
        return pl.BlockSpec((D // TALL, TALL, D), lambda i: (index(i), 0, 0))

    results = pl.pallas_call(
        finish_kernel,
        grid=(PARTS,),
        in_specs=[
            arrived, arrived, sums(lambda i: i), sums(lambda i: PARTS + i), sums(lambda i: jnp.minimum(i, last)),
            sums(lambda i: last + 1), pl.BlockSpec((8, D), lambda i: (0, 0)),
        ],
        out_specs=[
            placed, placed,
            pl.BlockSpec((D, D), lambda i: (0, jnp.minimum(i, last))), pl.BlockSpec((D, D), lambda i: (0, 0)),
            pl.BlockSpec((D, D), lambda i: (0, i)), pl.BlockSpec((D, D), lambda i: (i, 0)),
            pl.BlockSpec((D,), lambda i: (0,)), pl.BlockSpec((D,), lambda i: (0,)),
        ],
        out_shape=[
            shape(tile), shape(tile), shape((D, 3 * D), F32), shape((D, D), F32), shape((D, FF), F32),
            shape((FF, D), F32), shape((D,), F32), shape((D,), F32),
        ],
        compiler_params=pltpu.CompilerParams(vmem_limit_bytes=48 * 2**20),
    )(out_blocks, grad_blocks, total_mlp, total_mlp, total_rest, total_rest, total_gain)
    return tuple(result.reshape(activations.shape) for result in results[:2]) + tuple(results[2:])


def solution(mesh):
    tile = P("row", "col", None)
    return jax.shard_map(
        shards,
        mesh=mesh,
        in_specs=(tile, tile) + (P(),) * 6,
        out_specs=(tile, tile) + (P(),) * 6,
        check_vma=False,
    )
```

time: 238 us -> 214 us (0.90)
  Pallas kernels: 229 us -> 208 us
  local copies, waits for them, and re-layouts: 7.27 us -> 4.78 us
    pallas_call x1, Pallas kernels: 223 us -> 201 us  [shards(): pl.pallas_call(whole_kernel, in_specs=[WHOLE] * 8, out_specs=[WHOLE] * 5,...]
    broadcast_in_dim x2 -> x0, local copies, waits for them, and re-layouts: 2.49 us -> none  [the longest x1 1.25 us: shards(): first_gain[None, :]]
where the time goes in v4:
time: 214 us
  Pallas kernels  208 us (97%)
  local copies, waits for them, and re-layouts  4.78 us (2%)
    pallas_call x1, Pallas kernels, shards(): pl.pallas_call(whole_kernel, in_specs=[WHOLE] * 8, out_specs=[WHOLE] * 5,...  201 us
    pallas_call x1, Pallas kernels, shards(): pl.pallas_call(finish_kernel, grid=(PARTS,), in_specs=[arrived, arrived,...  7.05 us
    unnamed x8, local copies, waits for them, and re-layouts  4.78 us

profile of v4, /device:TPU:1, one launch (start us, length us, event | category | flops | bytes accessed | tf_op | source)
XLA Modules:
  0.0 213.9 jit_solution(17889334807395751695)
XLA Ops:
  0.6 201.4 %shard_map.143 = (bf16[2,128,8,384]{3,2,1,0:T(8,128)(2,1)}, bf16[2,128,8,384]{3,2,1,0:T(8,128)(2,1)}, bf16[192,16,384]{2,1,0:T(8,128)(2,1)}, bf16[96,16,384]{2,1,0:T(8,128)(2,1)}, f32[8,384]{1,0:T(8,128)}) custom-call(bf16[64,32,384]{2,1,0:T(8,128)(2,1)} %activations.1, bf16[64,32,384]{2,1,0:T(8,128)(2,1)} %cotangent.1, f32[384]{0:T(512)} %first_gain.1, ...), custom_call_target="tpu_custom_call" | custom-call | flops 120000004096 | bytes 100000000 | tf_op jit(solution)/shard_map/pallas_call | solution.py:571
  202.1 0.0 copy-start
  202.1 1.3 copy-done
  203.3 0.0 copy-start.1
  203.3 1.4 copy-done.1
  204.8 0.0 copy-start.2
  204.8 1.4 copy-done.2
  206.2 0.0 copy-start.3
  206.2 0.7 copy-done.3
  206.9 7.0 %shard_map.144 = (bf16[2,32,32,384]{3,2,1,0:T(8,128)(2,1)}, bf16[2,32,32,384]{3,2,1,0:T(8,128)(2,1)}, f32[384,1152]{1,0:T(8,128)}, f32[384,384]{1,0:T(8,128)}, f...) custom-call(bf16[2,128,8,384]{3,2,1,0:T(8,128)(2,1)S(1)} %copy-done.1, ...), custom_call_target="tpu_custom_call" | custom-call | tf_op jit(solution)/shard_map/pallas_call | solution.py:607
Async XLA Ops:
  202.1 1.3 copy-start
  203.3 1.4 copy-start.1
  204.8 1.4 copy-start.2
  206.2 0.7 copy-start.3

commit v5 on v4

--- a/solution.py
+++ b/solution.py
@@ -247,15 +247,25 @@
     def along(self, half, index):
         return (self.row, index * 2 + self.core) if half == 0 else (index, self.col)
 
-    def apart(self, step):
-        jump = lax.rem(step * 45, DEVICES)
-        x = lax.rem(lax.rem(self.row, 2) * 2 + self.col // 8 + (jump // 2) % 4, 4)
-        y = lax.rem((self.col // 2) % 4 + (jump // 8) % 4, 4)
-        z = lax.rem(self.row // 2 + jump // 32, 4)
-        core = lax.rem(self.core + jump % 2, 2)
-        row = z * 2 + x // 2
-        col = (x % 2) * 8 + y * 2 + core
-        return row, col
+    def visit(self, work):
+        z, y = lax.div(self.row, 2), lax.rem(lax.div(self.col, 2), 4)
+        x = lax.rem(self.row, 2) * 2 + lax.div(self.col, 8)
+        near = []
+        for jump in range(8):
+            to_x, to_core = lax.rem(x + jump // 2, 4), lax.rem(self.core + jump % 2, 2)
+            near.append((lax.div(to_x, 2), lax.rem(to_x, 2) * 8 + to_core))
+
+        def corner(z, y, first):
+            for row, col in near[first:]:
+                work(z * 2 + row, y * 2 + col)
+
+        def step(turn, carry):
+            jump = lax.rem(turn * 5, 16)
+            corner(lax.rem(z + lax.div(jump, 4), 4), lax.rem(y + lax.rem(jump, 4), 4), 0)
+            return carry
+
+        corner(z, y, 1)
+        lax.fori_loop(1, 16, step, 0)
 
 
 def remote(source, target, sems, index, device):
@@ -270,13 +280,11 @@
 
 
 def swap_start(place, packed, arrived, sems, which, half):
-    def send(step, carry):
-        row, col = place.apart(step)
+    def send(row, col):
         source, target = packed.at[half, row * 16 + col], arrived.at[half, place.me]
         remote(source, target, sems, which * 2 + half, (row, col)).start()
-        return carry
-
-    lax.fori_loop(1, DEVICES, send, 0)
+
+    place.visit(send)
     arrived[half, place.me] = packed[half, place.me]
 
 
@@ -394,11 +402,10 @@
     place = Place()
     barrier = pltpu.get_barrier_semaphore()
 
-    def greet(step, carry):
-        pl.semaphore_signal(barrier, inc=1, device_id=place.apart(step), device_id_type=MESH)
-        return carry
-
-    lax.fori_loop(1, DEVICES, greet, 0)
+    def greet(row, col):
+        pl.semaphore_signal(barrier, inc=1, device_id=(row, col), device_id_type=MESH)
+
+    place.visit(greet)
     pack(activations, packed_a)
     pl.semaphore_wait(barrier, DEVICES - 1)
     for half in range(2):
@@ -448,6 +455,9 @@
     sum_expand = sum_mlp.at[pl.ds(0, FF)]
     sum_reduce = sum_mlp.at[pl.ds(FF, FF)]
 
+    mlp = DeviceSum(place, sum_mlp, total_mlp, mlp_away, mlp_sibling, mlp_in_a, mlp_part, mlp_in_b, mlp_sems)
+    rest = DeviceSum(place, sum_rest, total_rest, rest_away, rest_sibling, rest_in_a, rest_part, rest_in_b, rest_sems)
+
     def middle(half):
         swap_wait(cot, swap_sems, 1, 1, half)
         spread(rows_b, cot, half)
@@ -459,19 +469,17 @@
             )
 
         groups_of(half, work)
+        pl.when(half == 1)(mlp.start)
         gather_rows(rows_a, packed_a, half)
         swap_start(place, packed_a, block_out, swap_sems, 2, half)
 
     by_halves(middle)
     for half in range(2):
         swap_wait(packed_b, swap_sems, 0, 1, half)
-    mlp = DeviceSum(place, sum_mlp, total_mlp, mlp_away, mlp_sibling, mlp_in_a, mlp_part, mlp_in_b, mlp_sems)
-    rest = DeviceSum(place, sum_rest, total_rest, rest_away, rest_sibling, rest_in_a, rest_part, rest_in_b, rest_sems)
-    mlp.start()
 
     def back(half):
         def attention(group):
-            for turn, work in ((1, mlp.round_a), (3, mlp.round_b), (5, mlp.round_c), (7, mlp.round_d)):
+            for turn, work in ((2, mlp.round_a), (4, mlp.round_b), (6, mlp.round_c)):
                 pl.when(group == turn)(work)
             attend_back_group(group, scaled_first, triple, stats, grad_mixed, grad_triple, sum_joint)
 
@@ -479,11 +487,13 @@
         pl.when(half == 1)(rest.start)
 
         def head(group):
-            pl.when(group == 7)(rest.round_a)
+            pl.when(group == 5)(mlp.round_d)
+            pl.when(group == 6)(rest.round_a)
             head_back_group(group, x_feat, grad_att, triple, gain_a, joint, rows_b, sum_first)
 
         groups_of(half, head)
         gather_rows(rows_b, packed_b, half)
+        pl.when(half == 1)(rest.round_b)
         swap_start(place, packed_b, grad_in, swap_sems, 3, half)
 
     by_halves(back)
@@ -508,7 +518,6 @@
         settle(slots.at[pl.ds(0, 7)], gain_sems, 1, index)
         return summed([slots[q] for q in range(8)])
 
-    rest.round_b()
     gain_first.wait()
     gain_round(gain_pair[0] + gain_pair[1], gain_x, 1, 0)
     rest.round_c()

time: 214 us -> 191 us (0.89)
  Pallas kernels: 208 us -> 185 us
    pallas_call x1, Pallas kernels: 201 us -> 178 us  [shards(): pl.pallas_call(whole_kernel, in_specs=[WHOLE] * 8, out_specs=[WHOLE] * 5,...]
where the time goes in v5:
time: 191 us; the launch traced here: 190 us
  Pallas kernels  185 us (97%)
  local copies, waits for them, and re-layouts  4.78 us (3%)
    pallas_call x1, Pallas kernels, shards(): pl.pallas_call(whole_kernel, in_specs=[WHOLE] * 8, out_specs=[WHOLE] * 5,...  178 us
    pallas_call x1, Pallas kernels, shards(): pl.pallas_call(finish_kernel, grid=(PARTS,), in_specs=[arrived, arrived,...  7.05 us
    unnamed x8, local copies, waits for them, and re-layouts  4.78 us

profile of v5, /device:TPU:1, one launch (start us, length us, event | category | flops | bytes accessed | tf_op | source)
XLA Modules:
  0.0 190.3 jit_solution(17197959914672119827)
XLA Ops:
  0.6 177.8 %shard_map.143 = (bf16[2,128,8,384]{3,2,1,0:T(8,128)(2,1)}, bf16[2,128,8,384]{3,2,1,0:T(8,128)(2,1)}, bf16[192,16,384]{2,1,0:T(8,128)(2,1)}, bf16[96,16,384]{2,1,0:T(8,128)(2,1)}, f32[8,384]{1,0:T(8,128)}) custom-call(bf16[64,32,384]{2,1,0:T(8,128)(2,1)} %activations.1, bf16[64,32,384]{2,1,0:T(8,128)(2,1)} %cotangent.1, f32[384]{0:T(512)} %first_gain.1, ...), custom_call_target="tpu_custom_call" | custom-call | flops 120000004096 | bytes 100000000 | tf_op jit(solution)/shard_map/pallas_call | solution.py:580
  178.4 0.0 copy-start
  178.4 1.3 copy-done
  179.7 0.0 copy-start.1
  179.7 1.4 copy-done.1
  181.1 0.0 copy-start.2
  181.1 1.4 copy-done.2
  182.5 0.0 copy-start.3
  182.5 0.7 copy-done.3
  183.2 7.0 %shard_map.144 = (bf16[2,32,32,384]{3,2,1,0:T(8,128)(2,1)}, bf16[2,32,32,384]{3,2,1,0:T(8,128)(2,1)}, f32[384,1152]{1,0:T(8,128)}, f32[384,384]{1,0:T(8,128)}, f...) custom-call(bf16[2,128,8,384]{3,2,1,0:T(8,128)(2,1)S(1)} %copy-done.1, ...), custom_call_target="tpu_custom_call" | custom-call | tf_op jit(solution)/shard_map/pallas_call | solution.py:616
Async XLA Ops:
  178.4 1.3 copy-start
  179.7 1.4 copy-start.1
  181.1 1.4 copy-start.2
  182.5 0.7 copy-start.3

commit v6 on v5

--- a/solution.py
+++ b/solution.py
@@ -407,21 +407,21 @@
 
     place.visit(greet)
     pack(activations, packed_a)
+    gain_a[...] = jnp.broadcast_to(first_gain[...].reshape(1, D), (TOKENS, D)).T
+    gain_b[...] = jnp.broadcast_to(second_gain[...].reshape(1, D), (TOKENS, D)).T
+    for sums in (sum_mlp, sum_rest, sum_first, sum_second):
+        sums[...] = jnp.zeros_like(sums)
     pl.semaphore_wait(barrier, DEVICES - 1)
     for half in range(2):
         swap_start(place, packed_a, act, swap_sems, 0, half)
     pack(cotangent, packed_b)
     for half in range(2):
         swap_start(place, packed_b, cot, swap_sems, 1, half)
-    gain_a[...] = jnp.broadcast_to(first_gain[...].reshape(1, D), (TOKENS, D)).T
-    gain_b[...] = jnp.broadcast_to(second_gain[...].reshape(1, D), (TOKENS, D)).T
     for natural, turned in ((joint, joint_t), (project, project_t), (expand, expand_t)):
         for start in range(0, natural.shape[1], D):
             turned[start : start + D, :] = natural[:, start : start + D].T
     for start in range(0, FF, D):
         reduce_t[:, start : start + D] = reduce[start : start + D, :].T
-    for sums in (sum_mlp, sum_rest, sum_first, sum_second):
-        sums[...] = jnp.zeros_like(sums)
 
     def by_halves(work):
         def step(half, carry):
@@ -477,30 +477,14 @@
     for half in range(2):
         swap_wait(packed_b, swap_sems, 0, 1, half)
 
-    def back(half):
-        def attention(group):
-            for turn, work in ((2, mlp.round_a), (4, mlp.round_b), (6, mlp.round_c)):
-                pl.when(group == turn)(work)
-            attend_back_group(group, scaled_first, triple, stats, grad_mixed, grad_triple, sum_joint)
-
-        groups_of(half, attention)
-        pl.when(half == 1)(rest.start)
-
-        def head(group):
-            pl.when(group == 5)(mlp.round_d)
-            pl.when(group == 6)(rest.round_a)
-            head_back_group(group, x_feat, grad_att, triple, gain_a, joint, rows_b, sum_first)
-
-        groups_of(half, head)
-        gather_rows(rows_b, packed_b, half)
-        pl.when(half == 1)(rest.round_b)
-        swap_start(place, packed_b, grad_in, swap_sems, 3, half)
-
-    by_halves(back)
-    both = [jnp.sum(sums[...].T, axis=0, keepdims=True) for sums in (sum_first, sum_second)]
-    gain_pair[0] = jnp.concatenate(both + [jnp.zeros((6, D), F32)], axis=0)
-    gain_first = remote(gain_pair.at[0], gain_pair.at[1], gain_sems, 0, place.other)
-    gain_first.start()
+    def attention(group, carry):
+        for turn, work in ((2, mlp.round_a), (4, mlp.round_b), (6, mlp.round_c)):
+            pl.when(group == turn)(work)
+        attend_back_group(group, scaled_first, triple, stats, grad_mixed, grad_triple, sum_joint)
+        return carry
+
+    lax.fori_loop(0, GROUPS, attention, 0)
+    rest.start()
 
     def gain_round(values, slots, index, half):
         slot = place.slots[half]
@@ -518,9 +502,32 @@
         settle(slots.at[pl.ds(0, 7)], gain_sems, 1, index)
         return summed([slots[q] for q in range(8)])
 
-    gain_first.wait()
-    gain_round(gain_pair[0] + gain_pair[1], gain_x, 1, 0)
-    rest.round_c()
+    def gain_copy():
+        return remote(gain_pair.at[0], gain_pair.at[1], gain_sems, 0, place.other)
+
+    def gain_start():
+        both = [jnp.sum(sums[...].T, axis=0, keepdims=True) for sums in (sum_first, sum_second)]
+        gain_pair[0] = jnp.concatenate(both + [jnp.zeros((6, D), F32)], axis=0)
+        gain_copy().start()
+
+    def gain_next():
+        gain_copy().wait()
+        gain_round(gain_pair[0] + gain_pair[1], gain_x, 1, 0)
+
+    def back(half):
+        def head(group):
+            for turn, work in ((1, mlp.round_d), (2, rest.round_a), (6, rest.round_c)):
+                pl.when(group == turn)(work)
+            head_back_group(group, x_feat, grad_att, triple, gain_a, joint, rows_b, sum_first)
+
+        groups_of(half, head)
+        pl.when(half == 1)(gain_start)
+        gather_rows(rows_b, packed_b, half)
+        pl.when(half == 0)(rest.round_b)
+        pl.when(half == 1)(gain_next)
+        swap_start(place, packed_b, grad_in, swap_sems, 3, half)
+
+    by_halves(back)
     gain_round(gain_sum(gain_x, 1), gain_y, 2, 1)
     rest.round_d()
     total_gain[...] = gain_sum(gain_y, 2)
@@ -630,7 +637,7 @@
             shape(tile), shape(tile), shape((D, 3 * D), F32), shape((D, D), F32), shape((D, FF), F32),
             shape((FF, D), F32), shape((D,), F32), shape((D,), F32),
         ],
-        compiler_params=pltpu.CompilerParams(vmem_limit_bytes=48 * 2**20),
+        compiler_params=pltpu.CompilerParams(vmem_limit_bytes=63 * 2**20),
     )(out_blocks, grad_blocks, total_mlp, total_mlp, total_rest, total_rest, total_gain)
     return tuple(result.reshape(activations.shape) for result in results[:2]) + tuple(results[2:])
 

time: 191 us -> 187 us (0.979)
  local copies, waits for them, and re-layouts: 4.78 us -> 0 us
    unnamed x8 -> x0, local copies, waits for them, and re-layouts: 4.78 us -> none
where the time goes in v6:
time: 187 us
  Pallas kernels  186 us (99%)
    pallas_call x1, Pallas kernels, shards(): pl.pallas_call(whole_kernel, in_specs=[WHOLE] * 8, out_specs=[WHOLE] * 5,...  178 us
    pallas_call x1, Pallas kernels, shards(): pl.pallas_call(finish_kernel, grid=(PARTS,), in_specs=[arrived, arrived,...  8.13 us

profile of v6, /device:TPU:1, one launch (start us, length us, event | category | flops | bytes accessed | tf_op | source)
XLA Modules:
  0.0 186.7 jit_solution(13689866191310052267)
XLA Ops:
  0.6 177.9 %shard_map.143 = (bf16[2,128,8,384]{3,2,1,0:T(8,128)(2,1)}, bf16[2,128,8,384]{3,2,1,0:T(8,128)(2,1)}, bf16[192,16,384]{2,1,0:T(8,128)(2,1)}, bf16[96,16,384]{2,1,0:T(8,128)(2,1)}, f32[8,384]{1,0:T(8,128)}) custom-call(bf16[64,32,384]{2,1,0:T(8,128)(2,1)} %activations.1, bf16[64,32,384]{2,1,0:T(8,128)(2,1)} %cotangent.1, f32[384]{0:T(512)} %first_gain.1, ...), custom_call_target="tpu_custom_call" | custom-call | flops 120000004096 | bytes 100000000 | tf_op jit(solution)/shard_map/pallas_call | solution.py:587
  178.6 8.1 %shard_map.144 = (bf16[2,32,32,384]{3,2,1,0:T(8,128)(2,1)}, bf16[2,32,32,384]{3,2,1,0:T(8,128)(2,1)}, f32[384,1152]{1,0:T(8,128)}, f32[384,384]{1,0:T(8,128)}, f...) custom-call(bf16[2,128,8,384]{3,2,1,0:T(8,128)(2,1)} %get-tuple-element.21.out_blocks, ...), custom_call_target="tpu_custom_call" | custom-call | tf_op jit(solution)/shard_map/pallas_call | solution.py:623

commit v7 on v6

--- a/solution.py
+++ b/solution.py
@@ -478,7 +478,7 @@
         swap_wait(packed_b, swap_sems, 0, 1, half)
 
     def attention(group, carry):
-        for turn, work in ((2, mlp.round_a), (4, mlp.round_b), (6, mlp.round_c)):
+        for turn, work in ((3, mlp.round_a), (5, mlp.round_b), (7, mlp.round_c)):
             pl.when(group == turn)(work)
         attend_back_group(group, scaled_first, triple, stats, grad_mixed, grad_triple, sum_joint)
         return carry
@@ -516,7 +516,7 @@
 
     def back(half):
         def head(group):
-            for turn, work in ((1, mlp.round_d), (2, rest.round_a), (6, rest.round_c)):
+            for turn, work in ((2, rest.round_a), (4, mlp.round_d), (6, rest.round_c)):
                 pl.when(group == turn)(work)
             head_back_group(group, x_feat, grad_att, triple, gain_a, joint, rows_b, sum_first)
 

time: 187 us -> 185 us (0.989)
  Pallas kernels: 186 us -> 184 us
    pallas_call x1, Pallas kernels: 178 us -> 176 us  [shards(): pl.pallas_call(whole_kernel, in_specs=[WHOLE] * 8, out_specs=[WHOLE] * 5,...]
where the time goes in v7:
time: 185 us
  Pallas kernels  184 us (99%)
    pallas_call x1, Pallas kernels, shards(): pl.pallas_call(whole_kernel, in_specs=[WHOLE] * 8, out_specs=[WHOLE] * 5,...  176 us
    pallas_call x1, Pallas kernels, shards(): pl.pallas_call(finish_kernel, grid=(PARTS,), in_specs=[arrived, arrived,...  8.13 us

profile of v7, /device:TPU:1, one launch (start us, length us, event | category | flops | bytes accessed | tf_op | source)
XLA Modules:
  0.0 184.7 jit_solution(11117460473655132309)
XLA Ops:
  0.6 176.0 %shard_map.143 = (bf16[2,128,8,384]{3,2,1,0:T(8,128)(2,1)}, bf16[2,128,8,384]{3,2,1,0:T(8,128)(2,1)}, bf16[192,16,384]{2,1,0:T(8,128)(2,1)}, bf16[96,16,384]{2,1,0:T(8,128)(2,1)}, f32[8,384]{1,0:T(8,128)}) custom-call(bf16[64,32,384]{2,1,0:T(8,128)(2,1)} %activations.1, bf16[64,32,384]{2,1,0:T(8,128)(2,1)} %cotangent.1, f32[384]{0:T(512)} %first_gain.1, ...), custom_call_target="tpu_custom_call" | custom-call | flops 120000004096 | bytes 100000000 | tf_op jit(solution)/shard_map/pallas_call | solution.py:587
  176.6 8.1 %shard_map.144 = (bf16[2,32,32,384]{3,2,1,0:T(8,128)(2,1)}, bf16[2,32,32,384]{3,2,1,0:T(8,128)(2,1)}, f32[384,1152]{1,0:T(8,128)}, f32[384,384]{1,0:T(8,128)}, f...) custom-call(bf16[2,128,8,384]{3,2,1,0:T(8,128)(2,1)} %get-tuple-element.21.out_blocks, ...), custom_call_target="tpu_custom_call" | custom-call | tf_op jit(solution)/shard_map/pallas_call | solution.py:623

commit v8 on v7

--- a/solution.py
+++ b/solution.py
@@ -288,6 +288,19 @@
     arrived[half, place.me] = packed[half, place.me]
 
 
+def swap_start_both(place, packed, arrived, sems, which):
+    def send(row, col):
+        source, target = packed.at[:, row * 16 + col], arrived.at[:, place.me]
+        remote(source, target, sems, which * 2, (row, col)).start()
+
+    place.visit(send)
+    arrived[:, place.me] = packed[:, place.me]
+
+
+def swap_wait_both(some, sems, side, which):
+    settle(some.at[:, pl.ds(0, DEVICES - 1)], sems, side, which * 2)
+
+
 def swap_wait(some, sems, side, which, half):
     settle(some.at[half, pl.ds(0, DEVICES - 1)], sems, side, which * 2 + half)
 
@@ -415,8 +428,7 @@
     for half in range(2):
         swap_start(place, packed_a, act, swap_sems, 0, half)
     pack(cotangent, packed_b)
-    for half in range(2):
-        swap_start(place, packed_b, cot, swap_sems, 1, half)
+    swap_start_both(place, packed_b, cot, swap_sems, 1)
     for natural, turned in ((joint, joint_t), (project, project_t), (expand, expand_t)):
         for start in range(0, natural.shape[1], D):
             turned[start : start + D, :] = natural[:, start : start + D].T
@@ -459,7 +471,6 @@
     rest = DeviceSum(place, sum_rest, total_rest, rest_away, rest_sibling, rest_in_a, rest_part, rest_in_b, rest_sems)
 
     def middle(half):
-        swap_wait(cot, swap_sems, 1, 1, half)
         spread(rows_b, cot, half)
 
         def work(group):
@@ -473,9 +484,9 @@
         gather_rows(rows_a, packed_a, half)
         swap_start(place, packed_a, block_out, swap_sems, 2, half)
 
+    swap_wait_both(cot, swap_sems, 1, 1)
     by_halves(middle)
-    for half in range(2):
-        swap_wait(packed_b, swap_sems, 0, 1, half)
+    swap_wait_both(packed_b, swap_sems, 0, 1)
 
     def attention(group, carry):
         for turn, work in ((3, mlp.round_a), (5, mlp.round_b), (7, mlp.round_c)):

time: 185 us -> 185 us (level)
  no operation moved by 1% of the time
where the time goes in v8:
time: 185 us
  Pallas kernels  184 us (99%)
    pallas_call x1, Pallas kernels, shards(): pl.pallas_call(whole_kernel, in_specs=[WHOLE] * 8, out_specs=[WHOLE] * 5,...  176 us
    pallas_call x1, Pallas kernels, shards(): pl.pallas_call(finish_kernel, grid=(PARTS,), in_specs=[arrived, arrived,...  8.13 us

profile of v8, /device:TPU:1, one launch (start us, length us, event | category | flops | bytes accessed | tf_op | source)
XLA Modules:
  0.0 184.7 jit_solution(17399140278937047997)
XLA Ops:
  0.6 175.9 %shard_map.143 = (bf16[2,128,8,384]{3,2,1,0:T(8,128)(2,1)}, bf16[2,128,8,384]{3,2,1,0:T(8,128)(2,1)}, bf16[192,16,384]{2,1,0:T(8,128)(2,1)}, bf16[96,16,384]{2,1,0:T(8,128)(2,1)}, f32[8,384]{1,0:T(8,128)}) custom-call(bf16[64,32,384]{2,1,0:T(8,128)(2,1)} %activations.1, bf16[64,32,384]{2,1,0:T(8,128)(2,1)} %cotangent.1, f32[384]{0:T(512)} %first_gain.1, ...), custom_call_target="tpu_custom_call" | custom-call | flops 120000004096 | bytes 100000000 | tf_op jit(solution)/shard_map/pallas_call | solution.py:598
  176.6 8.1 %shard_map.144 = (bf16[2,32,32,384]{3,2,1,0:T(8,128)(2,1)}, bf16[2,32,32,384]{3,2,1,0:T(8,128)(2,1)}, f32[384,1152]{1,0:T(8,128)}, f32[384,384]{1,0:T(8,128)}, f...) custom-call(bf16[2,128,8,384]{3,2,1,0:T(8,128)(2,1)} %get-tuple-element.21.out_blocks, ...), custom_call_target="tpu_custom_call" | custom-call | tf_op jit(solution)/shard_map/pallas_call | solution.py:634
